TPU v7x, 512 devices: a whole 4x4x16 slice. The times are simulated.
512 devices in a mesh: dp: 4 (over x), code: 128 (over y, z, core).
Axes of the slice: x: 4, y: 4, z: 16, core: 2. Of those that a mesh axis runs over, the one named last changes fastest.
Arguments:
- latents: bfloat16 [262144, 128], P(('dp', 'code')), may hold values from -6 to 6
- code_ids: int32 [262144], P(('dp', 'code')), may hold values from 0 to 65535, as said below
- ema_sums: float32 [65536, 128], P('code'), may hold values from -6 to 6
- ema_counts: float32 [65536], P('code'), may hold values from 0.5 to 16
- dead_codes: int32 [16384], P(('dp', 'code')), may hold values from 0 to 65535, as said below
- restart_index: int32 [16384], P(('dp', 'code')), may hold values from 0 to 511
- next_latents: bfloat16 [131072, 128], P(('dp', 'code')), may hold values from -6 to 6
Outputs:
- codebook: float32 [65536, 128], P('code')
- fresh_counts: float32 [65536], P('code')
- next_distance: float32 [131072], P(('dp', 'code'))
Inputs may be any that keep to these rules, and one draw needn't show every extreme that they name: `code_ids`: in each aligned block of 512 rows (the rows of one device) at most 12 ids lie in one range [o * 512, (o + 1) * 512), and some range holds exactly 12. `dead_codes`: all entries are distinct. In each aligned block of 32 entries (one device's) at most 1 codes lie in one range [o * 512, (o + 1) * 512), and some range holds exactly 1. `restart_index`: entry j names a row of the j // 32-th aligned block of 512 latents.
All inputs are finite; a program needn't handle non-finite values.
Results may differ from a plain program's by a relative error of at most 0.00035.
Values may be sent and summed in bfloat16 or wider, within the bound.
A program may use at most 64 MiB of HBM per device.

v0:
```python
import jax
import jax.numpy as jnp
from jax import lax
from jax.sharding import PartitionSpec as P

decay_rate = 0.8
block_rows = 512


def pack_rows(labels, row_data, slots, owners, k_dev):
    owner = labels // k_dev
    matches = (owner[:, None] == jnp.arange(owners, dtype=jnp.int32)[None, :]).astype(jnp.int32)
    ranking = jnp.sum((jnp.cumsum(matches, 0) - 1) * matches, 1)
    target = owner * slots + ranking
    width = row_data.shape[1]
    buffer = jnp.zeros((owners * slots, width), row_data.dtype).at[target].set(row_data)
    tags = jnp.full((owners * slots,), -1, jnp.int32).at[target].set(labels)
    return (buffer.reshape(owners, slots, width), tags.reshape(owners, slots))


def tally(tags, row_data, first_code, k_dev):
    offset = tags.reshape(-1) - first_code
    onehot = (offset[:, None] == jnp.arange(k_dev, dtype=jnp.int32)[None, :]).astype(jnp.bfloat16)
    flat = row_data.reshape(-1, row_data.shape[-1])
    sums = lax.dot_general(
        onehot, flat, (((0,), (0,)), ((), ())), preferred_element_type=jnp.float32
    )
    counts = jnp.sum(onehot, 0, dtype=jnp.float32)
    return (sums, counts)


def refresh(batch_sums, batch_counts, restart_rows, restart_flag, old_sums, old_counts):
    fresh_counts = decay_rate * old_counts + (1.0 - decay_rate) * batch_counts
    fresh_sums = decay_rate * old_sums + (1.0 - decay_rate) * batch_sums
    is_dead = restart_flag > 0.5
    fresh_counts = jnp.where(is_dead, jnp.ones_like(fresh_counts), fresh_counts)
    fresh_sums = jnp.where(is_dead[:, None], restart_rows, fresh_sums)
    return (fresh_sums / fresh_counts[:, None], fresh_counts)


def nearest_rows(piece, table, table_norms):
    width = piece.shape[1]

    def closest(query_block):
        scores = lax.dot_general(
            query_block, table, (((1,), (1,)), ((), ())), preferred_element_type=jnp.float32
        )
        return jnp.min(table_norms[None, :] - 2.0 * scores, 1)

    count_rows = piece.shape[0]
    blocks = piece.reshape(count_rows // block_rows, block_rows, width)
    return lax.map(closest, blocks).reshape(count_rows)


def per_device(latents, code_ids, ema_sums, ema_counts, dead_codes, restart_index, next_latents):
    owners = lax.axis_size("code")
    k_dev = ema_sums.shape[0]
    next_dev = next_latents.shape[0]
    width = latents.shape[1]
    capacity = 3 * latents.shape[0] // owners
    spare_slots = max(1, dead_codes.shape[0] // owners)
    first_code = lax.axis_index("code") * k_dev
    batch_rows, batch_tags = pack_rows(code_ids, latents, capacity, owners, k_dev)
    restart_data = jnp.take(latents, restart_index, axis=0)
    dead_rows, dead_tags = pack_rows(dead_codes, restart_data, spare_slots, owners, k_dev)
    joined_rows = jnp.concatenate([batch_rows, dead_rows], 1)
    joined_tags = jnp.concatenate([batch_tags, dead_tags], 1)
    joined_rows, joined_tags = (
        lax.all_to_all(joined_rows, "code", split_axis=0, concat_axis=0, tiled=True),
        lax.all_to_all(joined_tags, "code", split_axis=0, concat_axis=0, tiled=True),
    )
    got_rows = joined_rows[:, :capacity]
    got_tags = joined_tags[:, :capacity]
    got_dead = joined_rows[:, capacity:]
    got_dead_tags = joined_tags[:, capacity:]
    batch_sums, batch_counts = tally(got_tags, got_rows, first_code, k_dev)
    restart_rows, restart_flag = tally(got_dead_tags, got_dead, first_code, k_dev)
    total_sums, total_counts, total_rows, total_flag = lax.psum(
        (batch_sums, batch_counts, restart_rows, restart_flag), "dp"
    )
    codebook, fresh_counts = refresh(
        total_sums, total_counts, total_rows, total_flag, ema_sums, ema_counts
    )
    shaped = codebook.astype(jnp.bfloat16)
    widened = shaped.astype(jnp.float32)
    code_norms = jnp.sum(widened * widened, 1)
    partial_best = nearest_rows(
        lax.all_gather(next_latents, "code", axis=0, tiled=True), shaped, code_norms
    )
    lowest = lax.pmin(partial_best, "code")
    best = lax.dynamic_slice_in_dim(lowest, lax.axis_index("code") * next_dev, next_dev, 0)
    queries = next_latents.astype(jnp.float32)
    next_distance = (best + jnp.sum(queries * queries, 1)) / width
    return (codebook, fresh_counts, next_distance)


def solution(mesh):
    in_specs = (
        P(("dp", "code"), None),
        P(("dp", "code")),
        P("code", None),
        P("code"),
        P(("dp", "code")),
        P(("dp", "code")),
        P(("dp", "code"), None),
    )
    out_specs = (P("code", None), P("code"), P(("dp", "code")))
    return jax.shard_map(
        per_device, mesh=mesh, in_specs=in_specs, out_specs=out_specs, check_vma=False
    )
```

profile of v0, /device:TPU:1, one launch (start us, length us, event | category | flops | bytes accessed | tf_op | source)
XLA Modules:
  0.0 645.3 jit_solution(11565247992329444830)
XLA Ops:
  10.8 2.6 scatter_custom_fusion
  16.8 20.6 %all-to-all-start = ((s32[128,1,13]{2,1,0:T(1,128)}), s32[128,1,13]{2,1,0:T(1,128)S(1)}, u32[]{:S(2)}, u32[]{:S(2)}) async-start(s32[128,1,13]{2,1,0:T(1,128)} %bitcast.8), calls=%async_computation | async-start | bytes 131072 | tf_op jit(solution)/shard_map/all_to_all | solution.py:70
  38.7 2.2 scatter_custom_fusion.2
  43.0 9.3 %all-to-all-done = s32[128,1,13]{2,1,0:T(1,128)S(1)} async-done(((s32[128,1,13]{2,1,0:T(1,128)}), s32[128,1,13]{2,1,0:T(1,128)S(1)}, u32[]{:S(2)}, u32[]{:S(2)}) %all-to-all-start) | async-done | bytes 6688 | tf_op jit(solution)/shard_map/all_to_all | solution.py:70
  52.4 6.9 %all-to-all-start.1 = ((bf16[128,13,128]{2,1,0:T(8,128)(2,1)}), bf16[128,13,128]{2,1,0:T(8,128)(2,1)S(1)}, u32[]{:S(2)}, u32[]{:S(2)}) async-start(bf16[128,13,128]{2,1,0:T(8,128)(2,1)} %pad_maximum_fusion), calls=%async_computation.1 | async-start | bytes 1048576 | tf_op jit(solution)/shard_map/all_to_all | solution.py:69
  59.6 32.9 %all-to-all-done.1 = bf16[128,13,128]{2,1,0:T(8,128)(2,1)S(1)} async-done(((bf16[128,13,128]{2,1,0:T(8,128)(2,1)}), bf16[128,13,128]{2,1,0:T(8,128)(2,1)S(1)}, u32[]{:S(2)}, u32[]{:S(2)}) %all-to-all-start.1) | async-done | bytes 426016 | tf_op jit(solution)/shard_map/all_to_all | solution.py:69
  92.5 2.0 fusion.6
  96.8 8.5 %all-reduce = (f32[512]{0:T(512)S(1)}, f32[512]{0:T(512)S(1)}) all-reduce(f32[512]{0:T(512)S(1)} %convert_reduce_fusion.1, f32[512]{0:T(512)S(1)} %convert_reduce_fusion), channel_id=1, replica_groups=mesh['dp'=4,'code'=128] {'dp'}, use_global_device_ids=true, to_apply=%region_8.9 | all-reduce | flops 1024 | bytes 8192 | tf_op jit(solution)/shard_map/psum | solution.py:78
  105.3 38.9 %all-reduce.7.cloned.1.call-done = (f32[512,128]{1,0:T(8,128)}, f32[512,128]{1,0:T(8,128)}) async-done(((f32[512,128]{1,0:T(8,128)}, f32[512,128]{1,0:T(8,128)}), (f32[512,128]{1,0:T(8,128)}, f32[512,128]{1,0:T(8,128)})) %all-reduce.7.cloned.1.call-update) | async-done | bytes 524304 | tf_op jit(solution)/shard_map/psum | solution.py:78
  144.2 2.0 multiply_reduce_fusion
  146.1 93.6 %all-gather.2.cloned.1.call-done = bf16[32768,128]{1,0:T(8,128)(2,1)} async-done(((bf16[256,128]{1,0:T(8,128)(2,1)}), bf16[32768,128]{1,0:T(8,128)(2,1)}) %all-gather.2.cloned.1.call-update) | async-done | bytes 8388624 | tf_op jit(solution)/shard_map/all_gather | solution.py:88
  239.7 84.1 %while.10 = (s32[]{:T(128)}, f32[64,512]{1,0:T(8,128)S(1)}, f32[512]{0:T(512)S(1)}, bf16[64,512,128]{2,1,0:T(8,128)(2,1)}, bf16[512,128]{1,0:T(8,128)(2,1)S(1)}, /*index=5*/s32[]{:T(128)}, s32[]{:T(128)}) while((s32[]{:T(128)}, f32[64,512]{1,0:T(8,128)S(1)}, f32[512]{0:T(512)S(1)}, bf16[64,512,128]{2,1,0:T(8,128)(2,1)}, ...), condition=%wide.region_18.19_spmd, body=%wide.region_16.18_spmd.sunk | while | flops 67894784 | bytes 270929 | solution.py:52
  241.0 1.2 fusion.41
  242.3 1.2 fusion.41
  243.7 1.2 fusion.41
  245.0 1.2 fusion.41
  246.3 1.2 fusion.41
  247.6 1.2 fusion.41
  248.9 1.2 fusion.41
  250.2 1.2 fusion.41
  251.5 1.2 fusion.41
  252.9 1.2 fusion.41
  254.2 1.2 fusion.41
  256.8 1.2 fusion.41
  258.1 1.2 fusion.41
  259.4 1.2 fusion.41
  262.0 1.2 fusion.41
  264.7 1.2 fusion.41
  266.0 1.2 fusion.41
  267.3 1.2 fusion.41
  269.9 1.2 fusion.41
  271.2 1.2 fusion.41
  272.6 1.2 fusion.41
  275.2 1.2 fusion.41
  276.5 1.2 fusion.41
  277.8 1.2 fusion.41
  279.1 1.2 fusion.41
  280.4 1.2 fusion.41
  283.1 1.2 fusion.41
  284.4 1.2 fusion.41
  285.7 1.2 fusion.41
  288.3 1.2 fusion.41
  289.6 1.2 fusion.41
  290.9 1.2 fusion.41
  293.6 1.2 fusion.41
  294.9 1.2 fusion.41
  296.2 1.2 fusion.41
  297.5 1.2 fusion.41
  298.8 1.2 fusion.41
  301.5 1.2 fusion.41
  302.8 1.2 fusion.41
  304.1 1.2 fusion.41
  306.7 1.2 fusion.41
  308.0 1.2 fusion.41
  309.3 1.2 fusion.41
  312.0 1.2 fusion.41
  314.6 1.2 fusion.41
  315.9 1.2 fusion.41
  317.2 1.2 fusion.41
  319.9 1.2 fusion.41
  321.2 1.2 fusion.41
  322.5 1.2 fusion.41
  324.6 311.9 %all-reduce.5.cloned.1.call-done = f32[32768]{0:T(1024)} async-done(((f32[32768]{0:T(1024)}), f32[32768]{0:T(1024)}) %all-reduce.5.cloned.1.call-update) | async-done | bytes 131088 | tf_op jit(solution)/shard_map/pmin | solution.py:90
  636.5 1.3 add_multiply_fusion
  (133 shorter events, 34.1 us)
Async XLA Ops:
  8.0 33.1 %copy-start.2 = (bf16[512,128]{1,0:T(8,128)(2,1)S(1)}, bf16[512,128]{1,0:T(8,128)(2,1)}, u32[]{:S(2)}) copy-start(bf16[512,128]{1,0:T(8,128)(2,1)} %param.9) | copy-start | bytes 393220
  16.8 35.5 %all-to-all-start = ((s32[128,1,13]{2,1,0:T(1,128)}), s32[128,1,13]{2,1,0:T(1,128)S(1)}, u32[]{:S(2)}, u32[]{:S(2)}) async-start(s32[128,1,13]{2,1,0:T(1,128)} %bitcast.8), calls=%async_computation | async-start | bytes 131072 | tf_op jit(solution)/shard_map/all_to_all | solution.py:70
  41.1 64.2 %copy-start.4 = (f32[512]{0:T(512)S(1)}, f32[512]{0:T(512)}, u32[]{:S(2)}) copy-start(f32[512]{0:T(512)} %param.12) | copy-start | bytes 6148
  41.1 103.1 %copy-start.1 = (f32[512,128]{1,0:T(8,128)S(1)}, f32[512,128]{1,0:T(8,128)}, u32[]{:S(2)}) copy-start(f32[512,128]{1,0:T(8,128)} %param.11) | copy-start | bytes 786436
  52.4 40.1 %all-to-all-start.1 = ((bf16[128,13,128]{2,1,0:T(8,128)(2,1)}), bf16[128,13,128]{2,1,0:T(8,128)(2,1)S(1)}, u32[]{:S(2)}, u32[]{:S(2)}) async-start(bf16[128,13,128]{2,1,0:T(8,128)(2,1)} %pad_maximum_fusion), calls=%async_computation.1 | async-start | bytes 1048576 | tf_op jit(solution)/shard_map/all_to_all | solution.py:69
  59.2 84.9 %all-reduce.7.cloned.1.call-start = ((), (), s32[]{:S(2)}) async-start(), calls=%async_computation.4 | async-start | bytes 1048576 | tf_op jit(solution)/shard_map/psum | solution.py:78
  95.6 144.1 %all-gather.2.cloned.1.call-start = ((), (), s32[]{:S(2)}) async-start(), calls=%async_computation.2 | async-start | bytes 8454144 | tf_op jit(solution)/shard_map/all_gather | solution.py:88
  96.2 540.3 %all-reduce.5.cloned.1.call-start = ((), (), s32[]{:S(2)}) async-start(), calls=%async_computation.3 | async-start | bytes 262144 | tf_op jit(solution)/shard_map/pmin | solution.py:90
  105.3 219.2 %copy-start.3 = (f32[512]{0:T(512)}, f32[512]{0:T(512)S(1)}, u32[]{:S(2)}) copy-start(f32[512]{0:T(512)S(1)} %get-tuple-element.48) | copy-start | bytes 6148
  144.2 180.4 %copy-start = (bf16[256,128]{1,0:T(8,128)(2,1)S(1)}, bf16[256,128]{1,0:T(8,128)(2,1)}, u32[]{:S(2)}) copy-start(bf16[256,128]{1,0:T(8,128)(2,1)} %param.15) | copy-start | bytes 196612
Sparse Core Ops, SparseCore 0:
  95.8 48.3 all-reduce.6
Sparse Core Ops, SparseCore 1:
  99.3 140.4 all-gather.1
  324.6 311.9 all-reduce.4
where the time goes:
time: 648 us; the launch traced here: 645 us
  waiting for transfers between devices  487 us (75%)
  matrix products  81.4 us (13%)
  starting transfers between devices  27.5 us (4%)
  between operations  15.7 us (2%)
  other arithmetic  12.3 us (2%)
  local copies, waits for them, and re-layouts  11.1 us (2%)
  blocking collectives  8.47 us (1%)
    pmin x1, waiting for transfers between devices, per_device(): lowest = lax.pmin(partial_best, 'code')  312 us
    all_gather x1, waiting for transfers between devices, per_device(): lax.all_gather(next_latents, 'code', axis=0, tiled=True)  93.6 us
    dot_general x64, matrix products, closest(): lax.dot_general(query_block, table, (((1,), (1,)), ((), ())), preferred_e...  78.4 us
    psum x1, waiting for transfers between devices, per_device(): lax.psum((batch_sums, batch_counts, restart_rows, restart_flag), 'dp')  38.9 us
    all_to_all x1, waiting for transfers between devices, per_device(): lax.all_to_all(joined_rows, 'code', split_axis=0, concat_axis=0, tiled=True)  32.9 us
    all_to_all x1, starting transfers between devices, per_device(): lax.all_to_all(joined_tags, 'code', split_axis=0, concat_axis=0, tiled=True)  20.6 us
  transfers between devices with their start and end apart: 5, of which 5 were waited for; matrix products, arithmetic and copies ran while one was open for 1% of the time, Pallas kernels for 0%

commit v1 on v0

v1 whole, which is shorter than its diff:
```python
import functools

import jax
import jax.numpy as jnp
from jax import lax
from jax.experimental import pallas as pl
from jax.experimental.pallas import tpu as pltpu
from jax.sharding import PartitionSpec as P

MESH = pl.DeviceIdType.MESH
DECAY = 0.8
TILE = 16
DEAD_SLOT = 12
CORES = 2
BIG = 3.0e38
NT = (((1,), (1,)), ((), ()))


def onehot(mask):
    return jnp.where(mask, 1.0, 0.0).astype(jnp.bfloat16)


def column(row):
    return jnp.broadcast_to(row, (128, 128)).T


def body(
    nx, ny, nz, lat, ids, dead, ridx, ema_s, ema_c, nxt, book, cnt_out, dist,
    pack, zbuf, gbuf, qbuf, ext, rs_send, rs_recv, code, norm, acc, low_send, low_recv, cnts,
    z_s, z_r, g_s, g_r, q_s, q_r, f_s, f_r, x_s, x_r, b_s, b_r, c_s, c_r, right_s, right_r, left_s, left_r, m_s, m_r,
):
    rows = lat.shape[0]
    k_dev = book.shape[0]
    sub = k_dev // nx
    nyc = ny * CORES
    planes = nx * nyc
    group = nz // 4
    block = nyc * TILE
    shift_k = k_dev.bit_length() - 1
    shift_z = nz.bit_length() - 1

    x = lax.axis_index("dp")
    me = lax.axis_index("code")
    c = lax.rem(me, CORES)
    z = lax.rem(lax.div(me, CORES), nz)
    y = lax.div(me, CORES * nz)
    me_yc = y * CORES + c
    me_p = x * nyc + me_yc

    def at(ax, ay, az, ac):
        return (ax, (ay * nz + az) * CORES + ac)

    def in_plane(p):
        yc = lax.rem(p, nyc)
        return at(lax.div(p, nyc), lax.div(yc, CORES), z, lax.rem(yc, CORES))

    def along_z(d):
        return at(x, y, lax.rem(z + d + nz, nz), c)

    barrier = pltpu.get_barrier_semaphore()

    @pl.loop(1, planes)
    def _(d):
        pl.semaphore_signal(barrier, inc=1, device_id=in_plane(lax.rem(me_p + d, planes)), device_id_type=MESH)

    @pl.loop(1, nz)
    def _(d):
        pl.semaphore_signal(barrier, inc=1, device_id=along_z(d), device_id_type=MESH)

    lanes = rows + 128
    own = ids[...]

    def place(labels):
        owner = labels >> shift_k
        oc, oz, oy = owner & 1, (owner >> 1) & (nz - 1), owner >> (1 + shift_z)
        return oz * nyc + oy * CORES + oc

    owner = place(own)
    match = lax.broadcasted_iota(jnp.int32, (nyc * nz, rows), 0) == owner
    before = lax.broadcasted_iota(jnp.int32, (rows, rows), 0) < lax.broadcasted_iota(jnp.int32, (rows, rows), 1)
    earlier = jnp.dot(onehot(match), onehot(before), preferred_element_type=jnp.float32)
    rank = jnp.sum(jnp.where(match, earlier, 0.0), axis=0, keepdims=True).astype(jnp.int32)

    ext[...] = jnp.full(ext.shape, -1, jnp.int32)
    ext[0:1, 0 : dead.shape[1]] = dead[...]
    ext[1:2, 0 : dead.shape[1]] = ridx[...]
    gone = ext[0:1, :]
    gone_owner = jnp.where(gone >= 0, place(gone), -1024)
    pick = column(ext[1:2, :].astype(jnp.float32)).astype(jnp.int32)
    lane = lax.broadcasted_iota(jnp.int32, (128, 128), 1)
    picks = jnp.concatenate([onehot(pick == lane + 128 * i) for i in range(rows // 128)], axis=1)
    restarts = jnp.dot(picks, lat[...], preferred_element_type=jnp.float32).astype(jnp.bfloat16)
    data = jnp.concatenate([lat[...], restarts], axis=0)

    all_owner = jnp.concatenate([owner, gone_owner], axis=1)
    slot = jnp.concatenate([rank, jnp.full((1, 128), DEAD_SLOT, jnp.int32)], axis=1)
    tag = jnp.concatenate([(own & (k_dev - 1)) + 1, (gone & (k_dev - 1)) + (k_dev + 1)], axis=1)
    low = (tag & 31).astype(jnp.float32)
    high = (tag - (tag & 31)).astype(jnp.float32)
    key = all_owner * TILE + slot
    tag_key = all_owner * TILE + (DEAD_SLOT + 1)
    spot = onehot((lax.broadcasted_iota(jnp.int32, (128, lanes), 0) & (TILE - 1)) == slot)
    line = lax.broadcasted_iota(jnp.int32, (block, lanes), 0)
    lane_tile = lax.broadcasted_iota(jnp.int32, (1, 128), 1) >> 4

    def offset(k):
        return jnp.where(lax.rem(k, 2) == 1, lax.div(k + 1, 2), nz - lax.div(k, 2))

    def packed(k):
        base = lax.rem(z + offset(k), nz) * block
        put = onehot(line == key - base)
        moved = jnp.dot(put, data, preferred_element_type=jnp.float32)
        marks = jnp.where(line == tag_key - base, high, 0.0) + jnp.where(line == tag_key + 1 - base, low, 0.0)
        tags = lax.dot_general(marks.astype(jnp.bfloat16), spot, NT, preferred_element_type=jnp.float32)
        here = lax.rem(me_yc * nz + k, 8)
        tags = jnp.where(lane_tile == here, tags, 0.0)
        return (moved + tags).astype(jnp.bfloat16).reshape(nyc, TILE, 128)

    def z_copy(k):
        return pltpu.make_async_remote_copy(
            src_ref=pack.at[k], dst_ref=zbuf.at[k], send_sem=z_s.at[k], recv_sem=z_r.at[k],
            device_id=along_z(offset(k)), device_id_type=MESH,
        )

    pl.semaphore_wait(barrier, planes - 1 + nz - 1)

    @pl.loop(1, nz)
    def _(k):
        pack[k] = packed(k)
        z_copy(k).start()

    zbuf[0] = packed(jnp.int32(0))

    def xy_slot(i):
        return i * CORES + c

    def q_copy(i, slot_index):
        return pltpu.make_async_remote_copy(
            src_ref=nxt, dst_ref=qbuf.at[slot_index], send_sem=q_s.at[i], recv_sem=q_r.at[i],
            device_id=in_plane(xy_slot(i)), device_id_type=MESH,
        )

    spots = nx * ny
    me_xy = x * ny + y

    def q_send(i):
        return pltpu.make_async_remote_copy(
            src_ref=nxt, dst_ref=qbuf.at[me_p], send_sem=q_s.at[i], recv_sem=q_r.at[me_xy],
            device_id=in_plane(xy_slot(i)), device_id_type=MESH,
        )

    @pl.loop(1, spots)
    def _(d):
        q_send(lax.rem(me_xy + d, spots)).start()

    qbuf[me_p] = nxt[...]
    acc[...] = jnp.full(acc.shape, BIG, jnp.float32)
    wide = nxt[...].astype(jnp.float32)
    query_norm = jnp.sum((wide * wide).T, axis=0, keepdims=True)

    def g_copy(g, j):
        return pltpu.make_async_remote_copy(
            src_ref=zbuf.at[pl.ds(g * group, group), j],
            dst_ref=gbuf.at[me_yc, pl.ds(g * group, group)],
            send_sem=g_s.at[g, j], recv_sem=g_r.at[g, me_yc],
            device_id=at(x, lax.div(j, CORES), z, lax.rem(j, CORES)), device_id_type=MESH,
        )

    def g_got(g, j):
        return pltpu.make_async_remote_copy(
            src_ref=zbuf.at[pl.ds(g * group, group), j],
            dst_ref=gbuf.at[j, pl.ds(g * group, group)],
            send_sem=g_s.at[g, j], recv_sem=g_r.at[g, j],
            device_id=at(x, lax.div(j, CORES), z, lax.rem(j, CORES)), device_id_type=MESH,
        )

    @pl.loop(0, 4)
    def _(g):
        @pl.loop(g * group, (g + 1) * group)
        def _(k):
            @pl.when(k > 0)
            def _():
                z_copy(k).wait_recv()

        @pl.loop(1, nyc)
        def _(d):
            g_copy(g, lax.rem(me_yc + d, nyc)).start()

        gbuf[me_yc, pl.ds(g * group, group)] = zbuf[pl.ds(g * group, group), me_yc]

    def f_copy(i):
        return pltpu.make_async_remote_copy(
            src_ref=qbuf.at[xy_slot(i)], dst_ref=qbuf.at[xy_slot(i)], send_sem=f_s.at[i], recv_sem=f_r.at[i],
            device_id=at(x, y, z, 1 - c), device_id_type=MESH,
        )

    def f_got(i):
        other = i * CORES + 1 - c
        return pltpu.make_async_remote_copy(
            src_ref=qbuf.at[other], dst_ref=qbuf.at[other], send_sem=f_s.at[i], recv_sem=f_r.at[i],
            device_id=at(x, y, z, 1 - c), device_id_type=MESH,
        )

    f_copy(me_xy).start()

    @pl.loop(1, spots)
    def _(d):
        i = lax.rem(me_xy + d, spots)
        q_copy(i, xy_slot(i)).wait_recv()
        f_copy(i).start()

    @pl.loop(0, 4)
    def _(g):
        @pl.loop(1, nyc)
        def _(d):
            g_got(g, lax.rem(me_yc + d, nyc)).wait_recv()

    total = nyc * nz * TILE
    got = gbuf[...].reshape(total, 128)
    in_tile = lax.broadcasted_iota(jnp.int32, (8, 128), 1) & (TILE - 1)
    read = onehot(in_tile > DEAD_SLOT)
    tags = jnp.concatenate(
        [
            jnp.dot(read, got[i * 128 : (i + 1) * 128], preferred_element_type=jnp.float32)[0:1].astype(jnp.int32)
            for i in range(total // 128)
        ],
        axis=1,
    )
    ones = jnp.ones((total, 128), jnp.bfloat16)
    name = lax.broadcasted_iota(jnp.int32, (sub, total), 0)

    def x_copy(to, frm):
        return pltpu.make_async_remote_copy(
            src_ref=rs_send.at[to], dst_ref=rs_recv.at[frm], send_sem=x_s.at[to], recv_sem=x_r.at[frm],
            device_id=at(to, y, z, c), device_id_type=MESH,
        )

    def tally(to):
        mine = tags - (to * sub + 1)
        hits = jnp.concatenate([onehot(name == mine), onehot(name == mine - k_dev)], axis=0)
        sums = jnp.dot(hits, got, preferred_element_type=jnp.float32)
        count = jnp.dot(hits, ones, preferred_element_type=jnp.float32)
        is_dead = count[sub:] > 0.5
        return jnp.where(is_dead, sums[sub:], sums[:sub]), jnp.where(is_dead, -1.0, count[:sub])

    for d in range(1, nx + 1):
        to = lax.rem(x + d, nx)
        sums, count = tally(to)
        ref = rs_send if d < nx else rs_recv
        ref[to, 0:sub, :] = sums
        ref[to, sub : sub + 8, :] = count.T[0:8]
        if d < nx:
            x_copy(to, x).start()
    for d in range(1, nx):
        x_copy(lax.rem(x + d, nx), lax.rem(x + d, nx)).wait_recv()

    count = jnp.zeros((1, 128), jnp.float32)
    dead_row = jnp.zeros((1, 128), jnp.float32)
    sums = jnp.zeros((sub, 128), jnp.float32)
    restart = jnp.zeros((sub, 128), jnp.float32)
    for i in range(nx):
        part = rs_recv[i, sub : sub + 1, :]
        count += jnp.maximum(part, 0.0)
        dead_row = jnp.maximum(dead_row, -part)
        piece = rs_recv[i, 0:sub, :]
        sums += piece
        restart += jnp.where(column(part) < 0.0, piece, 0.0)
    fresh_row = DECAY * ema_c[pl.ds(x, 1), :] + (1.0 - DECAY) * count
    fresh_row = jnp.where(dead_row > 0.5, 1.0, fresh_row)
    mine = pl.ds(pl.multiple_of(x * sub, sub), sub)
    fresh = DECAY * ema_s[mine, :] + (1.0 - DECAY) * sums
    fresh = jnp.where(column(dead_row) > 0.5, restart, fresh)
    rows_out = fresh / column(fresh_row)
    code[0] = (-2.0 * rows_out.astype(jnp.bfloat16).astype(jnp.float32)).astype(jnp.bfloat16)

    def right(t):
        return pltpu.make_async_remote_copy(
            src_ref=code.at[jnp.maximum(2 * t - 1, 0)], dst_ref=code.at[2 * t + 1],
            send_sem=right_s.at[t], recv_sem=right_r.at[t], device_id=along_z(1), device_id_type=MESH,
        )

    def left(t):
        return pltpu.make_async_remote_copy(
            src_ref=code.at[2 * t], dst_ref=code.at[2 * t + 2],
            send_sem=left_s.at[t], recv_sem=left_r.at[t], device_id=along_z(-1), device_id_type=MESH,
        )

    right(jnp.int32(0)).start()
    left(jnp.int32(0)).start()

    book[mine, :] = rows_out
    cnts[x] = jnp.broadcast_to(fresh_row, (8, 128))

    def b_copy(to, frm):
        span = pl.ds(pl.multiple_of(frm * sub, sub), sub)
        return pltpu.make_async_remote_copy(
            src_ref=book.at[span], dst_ref=book.at[span], send_sem=b_s.at[to], recv_sem=b_r.at[frm],
            device_id=at(to, y, z, c), device_id_type=MESH,
        )

    def c_copy(to, frm):
        return pltpu.make_async_remote_copy(
            src_ref=cnts.at[frm], dst_ref=cnts.at[frm], send_sem=c_s.at[to], recv_sem=c_r.at[frm],
            device_id=at(to, y, z, c), device_id_type=MESH,
        )

    for d in range(1, nx):
        to = lax.rem(x + d, nx)
        b_copy(to, x).start()
        c_copy(to, x).start()

    @pl.loop(0, spots)
    def _(i):
        f_got(i).wait_recv()

    steps = nz // 2
    unroll = min(8, planes)

    @pl.loop(0, steps)
    def _(t):
        right(t).wait_recv()

        @pl.when(t < steps - 1)
        def _():
            right(t + 1).start()
            left(t).wait_recv()

        @pl.when(t < steps - 2)
        def _():
            left(t + 1).start()

        table = code[pl.ds(2 * t, 2)].reshape(2 * sub, 128)
        wide_table = table.astype(jnp.float32)
        norm[...] = jnp.broadcast_to(0.25 * jnp.sum(wide_table * wide_table, axis=1, keepdims=True), (2 * sub, 128))

        @pl.loop(0, planes // unroll)
        def _(o):
            for i in range(unroll):
                p = o * unroll + i
                score = lax.dot_general(
                    code[pl.ds(2 * t, 2)].reshape(2 * sub, 128), qbuf[p], NT, preferred_element_type=jnp.float32
                )
                queries = score.shape[1]
                lows = [
                    jnp.min((norm[...] + score[:, h * 128 : (h + 1) * 128]).reshape(2 * sub // 8, 8, 128), axis=0)
                    for h in range(queries // 128)
                ]
                acc[p] = jnp.minimum(acc[p], jnp.concatenate(lows, axis=1))

    def m_copy(to, frm):
        return pltpu.make_async_remote_copy(
            src_ref=low_send.at[to], dst_ref=low_recv.at[frm], send_sem=m_s.at[to], recv_sem=m_r.at[frm],
            device_id=in_plane(to), device_id_type=MESH,
        )

    halves = nxt.shape[0] // 128

    def lowest(p):
        small = jnp.min(acc[p], axis=0, keepdims=True)
        parts = [jnp.broadcast_to(small[:, h * 128 : (h + 1) * 128], (8 // halves, 128)) for h in range(halves)]
        return jnp.concatenate(parts, axis=0)

    @pl.loop(1, planes)
    def _(d):
        to = lax.rem(me_p + d, planes)
        low_send[to] = lowest(to)
        m_copy(to, me_p).start()

    low_recv[me_p] = lowest(me_p)

    @pl.loop(1, planes)
    def _(d):
        frm = lax.rem(me_p + d, planes)
        m_copy(frm, frm).wait_recv()

    best = jnp.min(low_recv[...], axis=0)
    for h in range(halves):
        first = h * (8 // halves)
        dist[h : h + 1, :] = (best[first : first + 1] + query_norm[:, h * 128 : (h + 1) * 128]) / 128

    for d in range(1, nx):
        frm = lax.rem(x + d, nx)
        b_copy(frm, frm).wait_recv()
        c_copy(frm, frm).wait_recv()
    for i in range(nx):
        cnt_out[i : i + 1, :] = cnts[i, 0:1, :]

    @pl.loop(1, nz)
    def _(k):
        z_copy(k).wait_send()

    @pl.loop(1, spots)
    def _(d):
        q_send(lax.rem(me_xy + d, spots)).wait_send()

    @pl.loop(0, spots)
    def _(i):
        f_copy(i).wait_send()

    @pl.loop(0, 4)
    def _(g):
        @pl.loop(1, nyc)
        def _(d):
            g_copy(g, lax.rem(me_yc + d, nyc)).wait_send()

    for d in range(1, nx):
        to = lax.rem(x + d, nx)
        x_copy(to, x).wait_send()
        b_copy(to, x).wait_send()
        c_copy(to, x).wait_send()

    @pl.loop(0, steps)
    def _(t):
        right(t).wait_send()

        @pl.when(t < steps - 1)
        def _():
            left(t).wait_send()

    @pl.loop(1, planes)
    def _(d):
        m_copy(lax.rem(me_p + d, planes), me_p).wait_send()


def per_device(nx, ny, nz, latents, code_ids, ema_sums, ema_counts, dead_codes, restart_index, next_latents):
    k_dev = ema_sums.shape[0]
    sub = k_dev // nx
    nyc = ny * CORES
    planes = nx * nyc
    queries = next_latents.shape[0]
    vmem = pl.BlockSpec(memory_space=pltpu.VMEM)
    dma = pltpu.SemaphoreType.DMA
    bf16, f32 = jnp.bfloat16, jnp.float32
    book, counts, dist = pl.pallas_call(
        functools.partial(body, nx, ny, nz),
        out_shape=(
            jax.ShapeDtypeStruct((k_dev, 128), f32),
            jax.ShapeDtypeStruct((nx, sub), f32),
            jax.ShapeDtypeStruct((queries // 128, 128), f32),
        ),
        in_specs=[vmem] * 7,
        out_specs=(vmem,) * 3,
        scratch_shapes=[
            pltpu.VMEM((nz, nyc, TILE, 128), bf16),
            pltpu.VMEM((nz, nyc, TILE, 128), bf16),
            pltpu.VMEM((nyc, nz, TILE, 128), bf16),
            pltpu.VMEM((planes, queries, 128), bf16),
            pltpu.VMEM((8, 128), jnp.int32),
            pltpu.VMEM((nx, sub + 8, 128), f32),
            pltpu.VMEM((nx, sub + 8, 128), f32),
            pltpu.VMEM((nz, sub, 128), bf16),
            pltpu.VMEM((2 * sub, 128), f32),
            pltpu.VMEM((planes, 8, queries), f32),
            pltpu.VMEM((planes, 8, 128), f32),
            pltpu.VMEM((planes, 8, 128), f32),
            pltpu.VMEM((nx, 8, 128), f32),
            dma((nz,)), dma((nz,)),
            dma((4, nyc)), dma((4, nyc)),
            dma((nx * ny,)), dma((nx * ny,)),
            dma((nx * ny,)), dma((nx * ny,)),
            dma((nx,)), dma((nx,)),
            dma((nx,)), dma((nx,)),
            dma((nx,)), dma((nx,)),
            dma((nz // 2,)), dma((nz // 2,)),
            dma((nz // 2,)), dma((nz // 2,)),
            dma((planes,)), dma((planes,)),
        ],
        compiler_params=pltpu.CompilerParams(
            collective_id=0, has_side_effects=True, vmem_limit_bytes=40 * 1024 * 1024
        ),
    )(
        latents, code_ids.reshape(1, -1), dead_codes.reshape(1, -1), restart_index.reshape(1, -1),
        ema_sums, ema_counts.reshape(nx, sub), next_latents,
    )
    return book, counts.reshape(-1), dist.reshape(-1)


def solution(mesh, ny=4):
    nx = mesh.shape["dp"]
    nz = mesh.shape["code"] // (CORES * ny)
    in_specs = (
        P(("dp", "code"), None),
        P(("dp", "code")),
        P("code", None),
        P("code"),
        P(("dp", "code")),
        P(("dp", "code")),
        P(("dp", "code"), None),
    )
    reorder = functools.partial(per_device, nx, ny, nz)
    return jax.shard_map(
        lambda a, b, s, n, d, r, q: reorder(a, b, s, n, d, r, q),
        mesh=mesh,
        in_specs=in_specs,
        out_specs=(P("code", None), P("code"), P(("dp", "code"))),
        check_vma=False,
    )
```

time: 648 us -> 100 us (0.15)
  waiting for transfers between devices: 487 us -> 0 us
  Pallas kernels: 0 us -> 94.1 us
  matrix products: 81.4 us -> 0 us
  starting transfers between devices: 27.5 us -> 0 us
  between operations: 15.7 us -> 0.68 us
  other arithmetic: 12.3 us -> 0 us
  blocking collectives: 8.47 us -> 0 us
    pmin x1 -> x0, waiting for transfers between devices: 312 us -> none  [per_device(): lowest = lax.pmin(partial_best, 'code')]
    pallas_call x0 -> x1, Pallas kernels: none -> 94.1 us  [per_device(): pl.pallas_call(functools.partial(body, nx, ny, nz), out_shape=(jax.ShapeD...]
    all_gather x1 -> x0, waiting for transfers between devices: 93.6 us -> none  [per_device(): lax.all_gather(next_latents, 'code', axis=0, tiled=True)]
    dot_general x66 -> x0, matrix products: 81.4 us -> none  [the longest x64 78.4 us: closest(): lax.dot_general(query_block, table, (((1,), (1,)), ((), ())), preferred_e...]
    all_to_all x2 -> x0, waiting for transfers between devices: 42.2 us -> none  [the longest x1 32.9 us: per_device(): lax.all_to_all(joined_rows, 'code', split_axis=0, concat_axis=0, tiled=True)]
    psum x1 -> x0, waiting for transfers between devices: 38.9 us -> none  [per_device(): lax.psum((batch_sums, batch_counts, restart_rows, restart_flag), 'dp')]
    all_to_all x2 -> x0, starting transfers between devices: 27.4 us -> none  [the longest x1 20.6 us: per_device(): lax.all_to_all(joined_tags, 'code', split_axis=0, concat_axis=0, tiled=True)]
    psum x1 -> x0, blocking collectives: 8.47 us -> none  [per_device(): lax.psum((batch_sums, batch_counts, restart_rows, restart_flag), 'dp')]
  transfers between devices with their start and end apart: 5 -> 0, of which waited for: 5 -> 0; matrix products, arithmetic and copies ran while one was open for 1% -> 0% of each run, Pallas kernels for 0% -> 0%
where the time goes in v1:
time: 100 us; the launch traced here: 99.9 us
  Pallas kernels  94.1 us (94%)
  local copies, waits for them, and re-layouts  5.21 us (5%)
    pallas_call x1, Pallas kernels, per_device(): pl.pallas_call(functools.partial(body, nx, ny, nz), out_shape=(jax.ShapeD...  94.1 us
    unnamed x17, local copies, waits for them, and re-layouts  5.21 us

profile of v1, /device:TPU:1, one launch (start us, length us, event | category | flops | bytes accessed | tf_op | source)
XLA Modules:
  0.0 99.9 jit_solution(17488950409803995024)
XLA Ops:
  0.6 0.0 copy-start.4
  0.6 0.0 copy-start.3
  0.7 0.0 copy-start.5
  0.7 0.0 copy-start.6
  0.7 0.6 copy-done.4
  1.3 0.0 copy-done.3
  1.3 0.0 copy-done.5
  1.3 0.0 copy-done.6
  1.3 0.0 copy-start
  1.3 0.9 copy-done
  2.3 0.0 copy-start.1
  2.3 0.9 copy-done.1
  3.2 0.0 copy-start.2
  3.2 0.8 copy-done.2
  4.0 94.1 %shard_map.94 = (f32[512,128]{1,0:T(8,128)S(1)}, f32[4,128]{1,0:T(4,128)S(1)}, f32[2,128]{1,0:T(2,128)S(1)}) custom-call(bf16[512,128]{1,0:T(8,128)(2,1)S(1)} %copy-done.1, s32[1,512]{1,0:T(1,128)S(1)} %bitcast.6, s32[1,32]{1,0:T(1,128)S(1)} %bitcast.10, s32[1,32]{1,0:T(1,128)S(1)} %bitcast.11, f32[512,128]{1,0:T(8,128)S(1)} %copy-done, ...), custom_call_target="tpu_custom_call" | custom-call | tf_op jit(solution)/shard_map/pallas_call | solution.py:434
  98.1 0.7 copy.13
  98.8 0.6 copy.14
  99.4 0.6 copy.15
Async XLA Ops:
  0.6 0.7 copy-start.4
  0.6 0.7 copy-start.3
  0.7 0.7 copy-start.5
  0.7 0.7 copy-start.6
  1.3 1.0 copy-start
  2.3 0.9 copy-start.1
  3.2 0.8 copy-start.2

commit v2 on v1

--- a/solution.py
+++ b/solution.py
@@ -13,7 +13,6 @@
 DEAD_SLOT = 12
 CORES = 2
 BIG = 3.0e38
-NT = (((1,), (1,)), ((), ()))
 
 
 def onehot(mask):
@@ -25,13 +24,15 @@
 
 
 def body(
-    nx, ny, nz, lat, ids, dead, ridx, ema_s, ema_c, nxt, book, cnt_out, dist,
-    pack, zbuf, gbuf, qbuf, ext, rs_send, rs_recv, code, norm, acc, low_send, low_recv, cnts,
+    nx, ny, nz, lat_in, ids_in, dead_in, ridx_in, ema_s_in, ema_c_in, nxt_in, book, cnt_out, dist,
+    lat, ids, dead, ridx, ema_s, ema_c, nxt, turned,
+    pack, zbuf, gbuf, qbuf, ext, rs_send, rs_recv, code, norm, acc, low_send, low_recv, cnts, in_s,
     z_s, z_r, g_s, g_r, q_s, q_r, f_s, f_r, x_s, x_r, b_s, b_r, c_s, c_r, right_s, right_r, left_s, left_r, m_s, m_r,
 ):
     rows = lat.shape[0]
     k_dev = book.shape[0]
     sub = k_dev // nx
+    queries = nxt.shape[0]
     nyc = ny * CORES
     planes = nx * nyc
     group = nz // 4
@@ -57,6 +58,15 @@
     def along_z(d):
         return at(x, y, lax.rem(z + d + nz, nz), c)
 
+    mine = pl.ds(pl.multiple_of(x * sub, sub), sub)
+    sources = (lat_in, ids_in, dead_in, ridx_in, nxt_in, ema_c_in, ema_s_in.at[mine])
+    loads = [
+        pltpu.make_async_copy(src, dst, in_s.at[i])
+        for i, (src, dst) in enumerate(zip(sources, (lat, ids, dead, ridx, nxt, ema_c, ema_s)))
+    ]
+    for load in loads:
+        load.start()
+
     barrier = pltpu.get_barrier_semaphore()
 
     @pl.loop(1, planes)
@@ -67,6 +77,8 @@
     def _(d):
         pl.semaphore_signal(barrier, inc=1, device_id=along_z(d), device_id_type=MESH)
 
+    for load in loads[:4]:
+        load.wait()
     lanes = rows + 128
     own = ids[...]
 
@@ -90,16 +102,16 @@
     lane = lax.broadcasted_iota(jnp.int32, (128, 128), 1)
     picks = jnp.concatenate([onehot(pick == lane + 128 * i) for i in range(rows // 128)], axis=1)
     restarts = jnp.dot(picks, lat[...], preferred_element_type=jnp.float32).astype(jnp.bfloat16)
-    data = jnp.concatenate([lat[...], restarts], axis=0)
 
     all_owner = jnp.concatenate([owner, gone_owner], axis=1)
     slot = jnp.concatenate([rank, jnp.full((1, 128), DEAD_SLOT, jnp.int32)], axis=1)
-    tag = jnp.concatenate([(own & (k_dev - 1)) + 1, (gone & (k_dev - 1)) + (k_dev + 1)], axis=1)
-    low = (tag & 31).astype(jnp.float32)
-    high = (tag - (tag & 31)).astype(jnp.float32)
+    tag = jnp.concatenate([own & (k_dev - 1), (gone & (k_dev - 1)) + k_dev], axis=1)
+    tag = jnp.left_shift(128 + (tag & 127), tag >> 7).astype(jnp.float32)
     key = all_owner * TILE + slot
     tag_key = all_owner * TILE + (DEAD_SLOT + 1)
-    spot = onehot((lax.broadcasted_iota(jnp.int32, (128, lanes), 0) & (TILE - 1)) == slot)
+    spot = jnp.where((lax.broadcasted_iota(jnp.int32, (128, lanes), 0) & (TILE - 1)) == slot, 1.0, 0.0)
+    spot = jnp.concatenate([spot[:, i * 128 : (i + 1) * 128].T for i in range(lanes // 128)], axis=0)
+    data = jnp.concatenate([jnp.concatenate([lat[...], restarts], axis=0), spot.astype(jnp.bfloat16)], axis=1)
     line = lax.broadcasted_iota(jnp.int32, (block, lanes), 0)
     lane_tile = lax.broadcasted_iota(jnp.int32, (1, 128), 1) >> 4
 
@@ -108,13 +120,12 @@
 
     def packed(k):
         base = lax.rem(z + offset(k), nz) * block
-        put = onehot(line == key - base)
-        moved = jnp.dot(put, data, preferred_element_type=jnp.float32)
-        marks = jnp.where(line == tag_key - base, high, 0.0) + jnp.where(line == tag_key + 1 - base, low, 0.0)
-        tags = lax.dot_general(marks.astype(jnp.bfloat16), spot, NT, preferred_element_type=jnp.float32)
+        put = jnp.where(line == key - base, 1.0, jnp.where(line == tag_key - base, tag, 0.0))
+        moved = jnp.dot(put.astype(jnp.bfloat16), data, preferred_element_type=jnp.float32)
         here = lax.rem(me_yc * nz + k, 8)
-        tags = jnp.where(lane_tile == here, tags, 0.0)
-        return (moved + tags).astype(jnp.bfloat16).reshape(nyc, TILE, 128)
+        tags = jnp.where(lane_tile == here, moved[:, 128:], 0.0)
+        is_tag = (lax.broadcasted_iota(jnp.int32, (block, 128), 0) & (TILE - 1)) > DEAD_SLOT
+        return jnp.where(is_tag, tags, moved[:, :128]).astype(jnp.bfloat16).reshape(nyc, TILE, 128)
 
     def z_copy(k):
         return pltpu.make_async_remote_copy(
@@ -124,19 +135,26 @@
 
     pl.semaphore_wait(barrier, planes - 1 + nz - 1)
 
-    @pl.loop(1, nz)
-    def _(k):
-        pack[k] = packed(k)
-        z_copy(k).start()
+    @pl.loop(0, (nz - 1) // 3)
+    def _(o):
+        for i in range(3):
+            k = 1 + o * 3 + i
+            pack[k] = packed(k)
+            z_copy(k).start()
 
     zbuf[0] = packed(jnp.int32(0))
+
+    loads[4].wait()
+    wide = nxt[...].astype(jnp.float32)
+    query_norm = jnp.sum((wide * wide).T, axis=0, keepdims=True)
+    turned[...] = wide.T.astype(jnp.bfloat16)
 
     def xy_slot(i):
         return i * CORES + c
 
     def q_copy(i, slot_index):
         return pltpu.make_async_remote_copy(
-            src_ref=nxt, dst_ref=qbuf.at[slot_index], send_sem=q_s.at[i], recv_sem=q_r.at[i],
+            src_ref=turned, dst_ref=qbuf.at[slot_index], send_sem=q_s.at[i], recv_sem=q_r.at[i],
             device_id=in_plane(xy_slot(i)), device_id_type=MESH,
         )
 
@@ -145,7 +163,7 @@
 
     def q_send(i):
         return pltpu.make_async_remote_copy(
-            src_ref=nxt, dst_ref=qbuf.at[me_p], send_sem=q_s.at[i], recv_sem=q_r.at[me_xy],
+            src_ref=turned, dst_ref=qbuf.at[me_p], send_sem=q_s.at[i], recv_sem=q_r.at[me_xy],
             device_id=in_plane(xy_slot(i)), device_id_type=MESH,
         )
 
@@ -153,10 +171,8 @@
     def _(d):
         q_send(lax.rem(me_xy + d, spots)).start()
 
-    qbuf[me_p] = nxt[...]
+    qbuf[me_p] = turned[...]
     acc[...] = jnp.full(acc.shape, BIG, jnp.float32)
-    wide = nxt[...].astype(jnp.float32)
-    query_norm = jnp.sum((wide * wide).T, axis=0, keepdims=True)
 
     def g_copy(g, j):
         return pltpu.make_async_remote_copy(
@@ -221,13 +237,13 @@
     read = onehot(in_tile > DEAD_SLOT)
     tags = jnp.concatenate(
         [
-            jnp.dot(read, got[i * 128 : (i + 1) * 128], preferred_element_type=jnp.float32)[0:1].astype(jnp.int32)
+            jnp.dot(read, got[i * 128 : (i + 1) * 128], preferred_element_type=jnp.float32)[0:1]
             for i in range(total // 128)
         ],
         axis=1,
     )
     ones = jnp.ones((total, 128), jnp.bfloat16)
-    name = lax.broadcasted_iota(jnp.int32, (sub, total), 0)
+    name = (lax.broadcasted_iota(jnp.int32, (sub, total), 0) + 128).astype(jnp.float32)
 
     def x_copy(to, frm):
         return pltpu.make_async_remote_copy(
@@ -236,8 +252,11 @@
         )
 
     def tally(to):
-        mine = tags - (to * sub + 1)
-        hits = jnp.concatenate([onehot(name == mine), onehot(name == mine - k_dev)], axis=0)
+        scale = jnp.float32(1.0)
+        for i in range(1, nx):
+            scale = jnp.where(to == i, 0.5**i, scale)
+        here = tags * scale
+        hits = jnp.concatenate([onehot(name == here), onehot(name == here * 0.5**nx)], axis=0)
         sums = jnp.dot(hits, got, preferred_element_type=jnp.float32)
         count = jnp.dot(hits, ones, preferred_element_type=jnp.float32)
         is_dead = count[sub:] > 0.5
@@ -265,10 +284,11 @@
         piece = rs_recv[i, 0:sub, :]
         sums += piece
         restart += jnp.where(column(part) < 0.0, piece, 0.0)
+    for load in loads[5:]:
+        load.wait()
     fresh_row = DECAY * ema_c[pl.ds(x, 1), :] + (1.0 - DECAY) * count
     fresh_row = jnp.where(dead_row > 0.5, 1.0, fresh_row)
-    mine = pl.ds(pl.multiple_of(x * sub, sub), sub)
-    fresh = DECAY * ema_s[mine, :] + (1.0 - DECAY) * sums
+    fresh = DECAY * ema_s[...] + (1.0 - DECAY) * sums
     fresh = jnp.where(column(dead_row) > 0.5, restart, fresh)
     rows_out = fresh / column(fresh_row)
     code[0] = (-2.0 * rows_out.astype(jnp.bfloat16).astype(jnp.float32)).astype(jnp.bfloat16)
@@ -313,8 +333,21 @@
     def _(i):
         f_got(i).wait_recv()
 
+    def m_copy(to, frm):
+        return pltpu.make_async_remote_copy(
+            src_ref=low_send.at[to], dst_ref=low_recv.at[frm], send_sem=m_s.at[to], recv_sem=m_r.at[frm],
+            device_id=in_plane(to), device_id_type=MESH,
+        )
+
+    halves = queries // 128
+
+    def lowest(p):
+        small = jnp.min(acc[p], axis=0, keepdims=True)
+        parts = [jnp.broadcast_to(small[:, h * 128 : (h + 1) * 128], (8 // halves, 128)) for h in range(halves)]
+        return jnp.concatenate(parts, axis=0)
+
     steps = nz // 2
-    unroll = min(8, planes)
+    unroll = min(16, planes // 2)
 
     @pl.loop(0, steps)
     def _(t):
@@ -329,42 +362,29 @@
         def _():
             left(t + 1).start()
 
-        table = code[pl.ds(2 * t, 2)].reshape(2 * sub, 128)
-        wide_table = table.astype(jnp.float32)
+        wide_table = code[pl.ds(2 * t, 2)].reshape(2 * sub, 128).astype(jnp.float32)
         norm[...] = jnp.broadcast_to(0.25 * jnp.sum(wide_table * wide_table, axis=1, keepdims=True), (2 * sub, 128))
 
         @pl.loop(0, planes // unroll)
         def _(o):
             for i in range(unroll):
-                p = o * unroll + i
-                score = lax.dot_general(
-                    code[pl.ds(2 * t, 2)].reshape(2 * sub, 128), qbuf[p], NT, preferred_element_type=jnp.float32
+                p = lax.rem(me_p + 1 + o * unroll + i, planes)
+                score = jnp.dot(
+                    code[pl.ds(2 * t, 2)].reshape(2 * sub, 128), qbuf[p], preferred_element_type=jnp.float32
                 )
-                queries = score.shape[1]
                 lows = [
                     jnp.min((norm[...] + score[:, h * 128 : (h + 1) * 128]).reshape(2 * sub // 8, 8, 128), axis=0)
-                    for h in range(queries // 128)
+                    for h in range(halves)
                 ]
                 acc[p] = jnp.minimum(acc[p], jnp.concatenate(lows, axis=1))
 
-    def m_copy(to, frm):
-        return pltpu.make_async_remote_copy(
-            src_ref=low_send.at[to], dst_ref=low_recv.at[frm], send_sem=m_s.at[to], recv_sem=m_r.at[frm],
-            device_id=in_plane(to), device_id_type=MESH,
-        )
-
-    halves = nxt.shape[0] // 128
-
-    def lowest(p):
-        small = jnp.min(acc[p], axis=0, keepdims=True)
-        parts = [jnp.broadcast_to(small[:, h * 128 : (h + 1) * 128], (8 // halves, 128)) for h in range(halves)]
-        return jnp.concatenate(parts, axis=0)
-
-    @pl.loop(1, planes)
-    def _(d):
-        to = lax.rem(me_p + d, planes)
-        low_send[to] = lowest(to)
-        m_copy(to, me_p).start()
+            @pl.when(t == steps - 1)
+            def _():
+                @pl.loop(o * unroll, jnp.minimum((o + 1) * unroll, planes - 1))
+                def _(i):
+                    to = lax.rem(me_p + 1 + i, planes)
+                    low_send[to] = lowest(to)
+                    m_copy(to, me_p).start()
 
     low_recv[me_p] = lowest(me_p)
 
@@ -428,6 +448,7 @@
     nyc = ny * CORES
     planes = nx * nyc
     queries = next_latents.shape[0]
+    hbm = pl.BlockSpec(memory_space=pl.ANY)
     vmem = pl.BlockSpec(memory_space=pltpu.VMEM)
     dma = pltpu.SemaphoreType.DMA
     bf16, f32 = jnp.bfloat16, jnp.float32
@@ -438,13 +459,21 @@
             jax.ShapeDtypeStruct((nx, sub), f32),
             jax.ShapeDtypeStruct((queries // 128, 128), f32),
         ),
-        in_specs=[vmem] * 7,
+        in_specs=[hbm] * 7,
         out_specs=(vmem,) * 3,
         scratch_shapes=[
+            pltpu.VMEM(latents.shape, bf16),
+            pltpu.VMEM((1, code_ids.shape[0]), jnp.int32),
+            pltpu.VMEM((1, dead_codes.shape[0]), jnp.int32),
+            pltpu.VMEM((1, dead_codes.shape[0]), jnp.int32),
+            pltpu.VMEM((sub, 128), f32),
+            pltpu.VMEM((nx, sub), f32),
+            pltpu.VMEM((queries, 128), bf16),
+            pltpu.VMEM((128, queries), bf16),
             pltpu.VMEM((nz, nyc, TILE, 128), bf16),
             pltpu.VMEM((nz, nyc, TILE, 128), bf16),
             pltpu.VMEM((nyc, nz, TILE, 128), bf16),
-            pltpu.VMEM((planes, queries, 128), bf16),
+            pltpu.VMEM((planes, 128, queries), bf16),
             pltpu.VMEM((8, 128), jnp.int32),
             pltpu.VMEM((nx, sub + 8, 128), f32),
             pltpu.VMEM((nx, sub + 8, 128), f32),
@@ -454,6 +483,7 @@
             pltpu.VMEM((planes, 8, 128), f32),
             pltpu.VMEM((planes, 8, 128), f32),
             pltpu.VMEM((nx, 8, 128), f32),
+            dma((7,)),
             dma((nz,)), dma((nz,)),
             dma((4, nyc)), dma((4, nyc)),
             dma((nx * ny,)), dma((nx * ny,)),
@@ -466,7 +496,7 @@
             dma((planes,)), dma((planes,)),
         ],
         compiler_params=pltpu.CompilerParams(
-            collective_id=0, has_side_effects=True, vmem_limit_bytes=40 * 1024 * 1024
+            collective_id=0, has_side_effects=True, vmem_limit_bytes=56 * 1024 * 1024
         ),
     )(
         latents, code_ids.reshape(1, -1), dead_codes.reshape(1, -1), restart_index.reshape(1, -1),

time: 100 us -> 97.2 us (0.972)
  local copies, waits for them, and re-layouts: 5.21 us -> 2.91 us
    unnamed x17 -> x7, local copies, waits for them, and re-layouts: 5.21 us -> 2.91 us
where the time goes in v2:
time: 97.2 us; the launch traced here: 97.1 us
  Pallas kernels  93.5 us (96%)
  local copies, waits for them, and re-layouts  2.91 us (3%)
    pallas_call x1, Pallas kernels, per_device(): pl.pallas_call(functools.partial(body, nx, ny, nz), out_shape=(jax.ShapeD...  93.5 us
    unnamed x7, local copies, waits for them, and re-layouts  2.91 us

profile of v2, /device:TPU:1, one launch (start us, length us, event | category | flops | bytes accessed | tf_op | source)
XLA Modules:
  0.0 97.1 jit_solution(8629761289755483718)
XLA Ops:
  0.6 93.5 %shard_map.94 = (f32[512,128]{1,0:T(8,128)}, f32[4,128]{1,0:T(4,128)}, f32[2,128]{1,0:T(2,128)}) custom-call(bf16[512,128]{1,0:T(8,128)(2,1)} %lat_in.1, s32[1,512]{1,0:T(1,128)} %bitcast.6, s32[1,32]{1,0:T(1,128)} %bitcast.10, s32[1,32]{1,0:T(1,128)} %bitcast.11, f32[512,128]{1,0:T(8,128)} %ema_s_in.1, f32[4,128]{1,0:T(4,128)} %bitcast.7, ...), custom_call_target="tpu_custom_call" | custom-call | tf_op jit(solution)/shard_map/pallas_call | solution.py:455
  94.1 0.0 copy-start
  94.1 1.7 %copy.13 = f32[512,128]{1,0:T(8,128)} copy(f32[512,128]{1,0:T(8,128)} %get-tuple-element.12) | data formatting | bytes 524288
  95.8 0.0 copy-done
  95.8 0.0 copy-start.1
  95.8 0.6 copy.14
  96.4 0.1 copy-done.1
  96.5 0.6 copy.15
Async XLA Ops:
  94.1 1.7 %copy-start = (f32[4,128]{1,0:T(4,128)S(1)}, f32[4,128]{1,0:T(4,128)}, u32[]{:S(2)}) copy-start(f32[4,128]{1,0:T(4,128)} %get-tuple-element.7) | copy-start | bytes 6148
  95.8 0.7 copy-start.1

commit v3 on v2

--- a/solution.py
+++ b/solution.py
@@ -10,6 +10,7 @@
 MESH = pl.DeviceIdType.MESH
 DECAY = 0.8
 TILE = 16
+USED = 14
 DEAD_SLOT = 12
 CORES = 2
 BIG = 3.0e38
@@ -26,8 +27,8 @@
 def body(
     nx, ny, nz, lat_in, ids_in, dead_in, ridx_in, ema_s_in, ema_c_in, nxt_in, book, cnt_out, dist,
     lat, ids, dead, ridx, ema_s, ema_c, nxt, turned,
-    pack, zbuf, gbuf, qbuf, ext, rs_send, rs_recv, code, norm, acc, low_send, low_recv, cnts, in_s,
-    z_s, z_r, g_s, g_r, q_s, q_r, f_s, f_r, x_s, x_r, b_s, b_r, c_s, c_r, right_s, right_r, left_s, left_r, m_s, m_r,
+    pack, zbuf, relay, gsrc, gbuf, qbuf, ext, rs_send, rs_recv, code, norm, acc, low_send, low_recv, cnts, in_s,
+    z_s, z_r, relay_s, relay_r, g_s, g_r, q_s, q_r, f_s, f_r, x_s, x_r, b_s, b_r, c_s, c_r, right_s, right_r, left_s, left_r, m_s, m_r,
 ):
     rows = lat.shape[0]
     k_dev = book.shape[0]
@@ -36,7 +37,7 @@
     nyc = ny * CORES
     planes = nx * nyc
     group = nz // 4
-    block = nyc * TILE
+    block = nyc * USED
     shift_k = k_dev.bit_length() - 1
     shift_z = nz.bit_length() - 1
 
@@ -107,25 +108,30 @@
     slot = jnp.concatenate([rank, jnp.full((1, 128), DEAD_SLOT, jnp.int32)], axis=1)
     tag = jnp.concatenate([own & (k_dev - 1), (gone & (k_dev - 1)) + k_dev], axis=1)
     tag = jnp.left_shift(128 + (tag & 127), tag >> 7).astype(jnp.float32)
-    key = all_owner * TILE + slot
-    tag_key = all_owner * TILE + (DEAD_SLOT + 1)
+    local = all_owner & (nyc - 1)
+    goal = all_owner >> (nyc.bit_length() - 1)
+    key = local * (USED - 1) + slot
+    tag_key = local + nyc * (USED - 1)
     spot = jnp.where((lax.broadcasted_iota(jnp.int32, (128, lanes), 0) & (TILE - 1)) == slot, 1.0, 0.0)
     spot = jnp.concatenate([spot[:, i * 128 : (i + 1) * 128].T for i in range(lanes // 128)], axis=0)
     data = jnp.concatenate([jnp.concatenate([lat[...], restarts], axis=0), spot.astype(jnp.bfloat16)], axis=1)
     line = lax.broadcasted_iota(jnp.int32, (block, lanes), 0)
     lane_tile = lax.broadcasted_iota(jnp.int32, (1, 128), 1) >> 4
 
+    half = nz // 2
+    way = 1 - 2 * c
+
     def offset(k):
-        return jnp.where(lax.rem(k, 2) == 1, lax.div(k + 1, 2), nz - lax.div(k, 2))
+        return jnp.where(lax.rem(k, 2) == 1, half - lax.div(k + 1, 2), nz - half + lax.div(k, 2))
 
     def packed(k):
-        base = lax.rem(z + offset(k), nz) * block
-        put = jnp.where(line == key - base, 1.0, jnp.where(line == tag_key - base, tag, 0.0))
+        to = goal == lax.rem(z + offset(k), nz)
+        put = jnp.where(line == jnp.where(to, key, -1), 1.0, jnp.where(line == jnp.where(to, tag_key, -1), tag, 0.0))
         moved = jnp.dot(put.astype(jnp.bfloat16), data, preferred_element_type=jnp.float32)
         here = lax.rem(me_yc * nz + k, 8)
         tags = jnp.where(lane_tile == here, moved[:, 128:], 0.0)
-        is_tag = (lax.broadcasted_iota(jnp.int32, (block, 128), 0) & (TILE - 1)) > DEAD_SLOT
-        return jnp.where(is_tag, tags, moved[:, :128]).astype(jnp.bfloat16).reshape(nyc, TILE, 128)
+        is_tag = lax.broadcasted_iota(jnp.int32, (block, 128), 0) >= nyc * (USED - 1)
+        return jnp.where(is_tag, tags, moved[:, :128]).astype(jnp.bfloat16)
 
     def z_copy(k):
         return pltpu.make_async_remote_copy(
@@ -133,16 +139,35 @@
             device_id=along_z(offset(k)), device_id_type=MESH,
         )
 
+    def relay_in():
+        return pltpu.make_async_remote_copy(
+            src_ref=pack.at[0], dst_ref=relay, send_sem=z_s.at[0], recv_sem=relay_r,
+            device_id=along_z(way), device_id_type=MESH,
+        )
+
+    def relay_out():
+        return pltpu.make_async_remote_copy(
+            src_ref=relay, dst_ref=zbuf.at[0], send_sem=relay_s, recv_sem=z_r.at[0],
+            device_id=along_z(way * (half - 1)), device_id_type=MESH,
+        )
+
+    pack[0] = packed(jnp.int32(0))
     pl.semaphore_wait(barrier, planes - 1 + nz - 1)
-
-    @pl.loop(0, (nz - 1) // 3)
+    relay_in().start()
+
+    @pl.loop(0, half - 1)
     def _(o):
-        for i in range(3):
-            k = 1 + o * 3 + i
+        for i in range(2):
+            k = 1 + o * 2 + i
             pack[k] = packed(k)
             z_copy(k).start()
 
-    zbuf[0] = packed(jnp.int32(0))
+        @pl.when(o == (half - 1) // 2)
+        def _():
+            relay_in().wait_recv()
+            relay_out().start()
+
+    zbuf[nz - 1] = packed(jnp.int32(nz - 1))
 
     loads[4].wait()
     wide = nxt[...].astype(jnp.float32)
@@ -176,7 +201,7 @@
 
     def g_copy(g, j):
         return pltpu.make_async_remote_copy(
-            src_ref=zbuf.at[pl.ds(g * group, group), j],
+            src_ref=gsrc.at[pl.ds(g * group, group), j],
             dst_ref=gbuf.at[me_yc, pl.ds(g * group, group)],
             send_sem=g_s.at[g, j], recv_sem=g_r.at[g, me_yc],
             device_id=at(x, lax.div(j, CORES), z, lax.rem(j, CORES)), device_id_type=MESH,
@@ -184,25 +209,33 @@
 
     def g_got(g, j):
         return pltpu.make_async_remote_copy(
-            src_ref=zbuf.at[pl.ds(g * group, group), j],
+            src_ref=gsrc.at[pl.ds(g * group, group), j],
             dst_ref=gbuf.at[j, pl.ds(g * group, group)],
             send_sem=g_s.at[g, j], recv_sem=g_r.at[g, j],
             device_id=at(x, lax.div(j, CORES), z, lax.rem(j, CORES)), device_id_type=MESH,
         )
 
+    row = lax.broadcasted_iota(jnp.int32, (nyc * TILE, block), 0)
+    tile, spare = row >> 4, (row & (TILE - 1)) - DEAD_SLOT
+    origin = jnp.where(spare <= 0, tile * (USED - 1) + DEAD_SLOT + spare, jnp.where(spare == 1, tile + nyc * (USED - 1), -1))
+    spread = onehot(lax.broadcasted_iota(jnp.int32, (nyc * TILE, block), 1) == origin)
+
     @pl.loop(0, 4)
     def _(g):
-        @pl.loop(g * group, (g + 1) * group)
+        @pl.loop(g * group, jnp.minimum((g + 1) * group, nz - 1))
         def _(k):
-            @pl.when(k > 0)
-            def _():
-                z_copy(k).wait_recv()
+            z_copy(k).wait_recv()
+
+        for i in range(group):
+            k = g * group + i
+            tiles = jnp.dot(spread, zbuf[k], preferred_element_type=jnp.float32)
+            gsrc[k] = tiles.astype(jnp.bfloat16).reshape(nyc, TILE, 128)
 
         @pl.loop(1, nyc)
         def _(d):
             g_copy(g, lax.rem(me_yc + d, nyc)).start()
 
-        gbuf[me_yc, pl.ds(g * group, group)] = zbuf[pl.ds(g * group, group), me_yc]
+        gbuf[me_yc, pl.ds(g * group, group)] = gsrc[pl.ds(g * group, group), me_yc]
 
     def f_copy(i):
         return pltpu.make_async_remote_copy(
@@ -405,7 +438,10 @@
     for i in range(nx):
         cnt_out[i : i + 1, :] = cnts[i, 0:1, :]
 
-    @pl.loop(1, nz)
+    relay_in().wait_send()
+    relay_out().wait_send()
+
+    @pl.loop(1, nz - 1)
     def _(k):
         z_copy(k).wait_send()
 
@@ -440,6 +476,15 @@
     @pl.loop(1, planes)
     def _(d):
         m_copy(lax.rem(me_p + d, planes), me_p).wait_send()
+
+
+def hand_over(book, counts, dist, book_out, counts_out, dist_out, sem):
+    pairs = ((book, book_out), (counts, counts_out), (dist, dist_out))
+    copies = [pltpu.make_async_copy(src, dst, sem.at[i]) for i, (src, dst) in enumerate(pairs)]
+    for copy in copies:
+        copy.start()
+    for copy in copies:
+        copy.wait()
 
 
 def per_device(nx, ny, nz, latents, code_ids, ema_sums, ema_counts, dead_codes, restart_index, next_latents):
@@ -470,7 +515,9 @@
             pltpu.VMEM((nx, sub), f32),
             pltpu.VMEM((queries, 128), bf16),
             pltpu.VMEM((128, queries), bf16),
-            pltpu.VMEM((nz, nyc, TILE, 128), bf16),
+            pltpu.VMEM((nz, nyc * USED, 128), bf16),
+            pltpu.VMEM((nz, nyc * USED, 128), bf16),
+            pltpu.VMEM((nyc * USED, 128), bf16),
             pltpu.VMEM((nz, nyc, TILE, 128), bf16),
             pltpu.VMEM((nyc, nz, TILE, 128), bf16),
             pltpu.VMEM((planes, 128, queries), bf16),
@@ -485,6 +532,7 @@
             pltpu.VMEM((nx, 8, 128), f32),
             dma((7,)),
             dma((nz,)), dma((nz,)),
+            dma, dma,
             dma((4, nyc)), dma((4, nyc)),
             dma((nx * ny,)), dma((nx * ny,)),
             dma((nx * ny,)), dma((nx * ny,)),
@@ -502,7 +550,18 @@
         latents, code_ids.reshape(1, -1), dead_codes.reshape(1, -1), restart_index.reshape(1, -1),
         ema_sums, ema_counts.reshape(nx, sub), next_latents,
     )
-    return book, counts.reshape(-1), dist.reshape(-1)
+    return pl.pallas_call(
+        hand_over,
+        out_shape=(
+            jax.ShapeDtypeStruct((k_dev, 128), f32),
+            jax.ShapeDtypeStruct((k_dev,), f32),
+            jax.ShapeDtypeStruct((queries,), f32),
+        ),
+        in_specs=[hbm] * 3,
+        out_specs=(hbm,) * 3,
+        scratch_shapes=[dma((3,))],
+        compiler_params=pltpu.CompilerParams(vmem_limit_bytes=56 * 1024 * 1024),
+    )(book, counts.reshape(-1), dist.reshape(-1))
 
 
 def solution(mesh, ny=4):

time: 97.2 us -> 100 us (1.029)
  Pallas kernels: 93.5 us -> 99.7 us
  local copies, waits for them, and re-layouts: 2.91 us -> 0 us
    pallas_call x0 -> x1, Pallas kernels: none -> 9.16 us  [per_device(): pl.pallas_call(hand_over, out_shape=(jax.ShapeDtypeStruct((k_dev, 128), f...]
    pallas_call x1, Pallas kernels: 93.5 us -> 90.5 us  [per_device(): pl.pallas_call(functools.partial(body, nx, ny, nz), out_shape=(jax.ShapeD...]
    unnamed x7 -> x0, local copies, waits for them, and re-layouts: 2.91 us -> none
where the time goes in v3:
time: 100 us
  Pallas kernels  99.7 us (100%)
    pallas_call x1, Pallas kernels, per_device(): pl.pallas_call(functools.partial(body, nx, ny, nz), out_shape=(jax.ShapeD...  90.5 us
    pallas_call x1, Pallas kernels, per_device(): pl.pallas_call(hand_over, out_shape=(jax.ShapeDtypeStruct((k_dev, 128), f...  9.16 us

profile of v3, /device:TPU:1, one launch (start us, length us, event | category | flops | bytes accessed | tf_op | source)
XLA Modules:
  0.0 100.3 jit_solution(8001856764978304695)
XLA Ops:
  0.6 90.5 %shard_map.94 = (f32[512,128]{1,0:T(8,128)}, f32[4,128]{1,0:T(4,128)}, f32[2,128]{1,0:T(2,128)}) custom-call(bf16[512,128]{1,0:T(8,128)(2,1)} %lat_in.1, s32[1,512]{1,0:T(1,128)} %bitcast.6, s32[1,32]{1,0:T(1,128)} %bitcast.10, s32[1,32]{1,0:T(1,128)} %bitcast.11, f32[512,128]{1,0:T(8,128)} %ema_s_in.1, f32[4,128]{1,0:T(4,128)} %bitcast.7, ...), custom_call_target="tpu_custom_call" | custom-call | tf_op jit(solution)/shard_map/pallas_call | solution.py:500
  91.2 9.2 %shard_map.95 = (f32[512,128]{1,0:T(8,128)}, f32[512]{0:T(512)}, f32[256]{0:T(256)}) custom-call(f32[512,128]{1,0:T(8,128)} %get-tuple-element.6.book, f32[512]{0:T(512)} %bitcast.8, f32[256]{0:T(256)} %bitcast.9), custom_call_target="tpu_custom_call" | custom-call | tf_op jit(solution)/shard_map/pallas_call | solution.py:553

commit v4 on v3

--- a/solution.py
+++ b/solution.py
@@ -28,7 +28,8 @@
     nx, ny, nz, lat_in, ids_in, dead_in, ridx_in, ema_s_in, ema_c_in, nxt_in, book, cnt_out, dist,
     lat, ids, dead, ridx, ema_s, ema_c, nxt, turned,
     pack, zbuf, relay, gsrc, gbuf, qbuf, ext, rs_send, rs_recv, code, norm, acc, low_send, low_recv, cnts, in_s,
-    z_s, z_r, relay_s, relay_r, g_s, g_r, q_s, q_r, f_s, f_r, x_s, x_r, b_s, b_r, c_s, c_r, right_s, right_r, left_s, left_r, m_s, m_r,
+    z_s, z_r, relay_s, relay_r, g_s, g_r, qy_s, qy_r, qx_s, qx_r, f_s, f_r, x_s, x_r, b_s, b_r, c_s, c_r,
+    right_s, right_r, left_s, left_r, m_s, m_r,
 ):
     rows = lat.shape[0]
     k_dev = book.shape[0]
@@ -55,6 +56,9 @@
     def in_plane(p):
         yc = lax.rem(p, nyc)
         return at(lax.div(p, nyc), lax.div(yc, CORES), z, lax.rem(yc, CORES))
+
+    def sent(ref, sem):
+        pltpu.make_async_copy(ref, ref, sem).wait()
 
     def along_z(d):
         return at(x, y, lax.rem(z + d + nz, nz), c)
@@ -135,13 +139,13 @@
 
     def z_copy(k):
         return pltpu.make_async_remote_copy(
-            src_ref=pack.at[k], dst_ref=zbuf.at[k], send_sem=z_s.at[k], recv_sem=z_r.at[k],
+            src_ref=pack.at[k], dst_ref=zbuf.at[k], send_sem=z_s, recv_sem=z_r.at[lax.div(k, group)],
             device_id=along_z(offset(k)), device_id_type=MESH,
         )
 
     def relay_in():
         return pltpu.make_async_remote_copy(
-            src_ref=pack.at[0], dst_ref=relay, send_sem=z_s.at[0], recv_sem=relay_r,
+            src_ref=pack.at[0], dst_ref=relay, send_sem=z_s, recv_sem=relay_r,
             device_id=along_z(way), device_id_type=MESH,
         )
 
@@ -174,44 +178,34 @@
     query_norm = jnp.sum((wide * wide).T, axis=0, keepdims=True)
     turned[...] = wide.T.astype(jnp.bfloat16)
 
-    def xy_slot(i):
-        return i * CORES + c
-
-    def q_copy(i, slot_index):
-        return pltpu.make_async_remote_copy(
-            src_ref=turned, dst_ref=qbuf.at[slot_index], send_sem=q_s.at[i], recv_sem=q_r.at[i],
-            device_id=in_plane(xy_slot(i)), device_id_type=MESH,
-        )
-
-    spots = nx * ny
-    me_xy = x * ny + y
-
-    def q_send(i):
-        return pltpu.make_async_remote_copy(
-            src_ref=turned, dst_ref=qbuf.at[me_p], send_sem=q_s.at[i], recv_sem=q_r.at[me_xy],
-            device_id=in_plane(xy_slot(i)), device_id_type=MESH,
-        )
-
-    @pl.loop(1, spots)
-    def _(d):
-        q_send(lax.rem(me_xy + d, spots)).start()
-
-    qbuf[me_p] = turned[...]
+    def qy_copy(to):
+        return pltpu.make_async_remote_copy(
+            src_ref=turned, dst_ref=qbuf.at[x, y, c], send_sem=qy_s, recv_sem=qy_r,
+            device_id=at(x, to, z, c), device_id_type=MESH,
+        )
+
+    def qx_copy(to):
+        return pltpu.make_async_remote_copy(
+            src_ref=qbuf.at[x, :, c], dst_ref=qbuf.at[x, :, c], send_sem=qx_s, recv_sem=qx_r,
+            device_id=at(to, y, z, c), device_id_type=MESH,
+        )
+
+    def f_copy():
+        return pltpu.make_async_remote_copy(
+            src_ref=qbuf.at[:, :, c], dst_ref=qbuf.at[:, :, c], send_sem=f_s, recv_sem=f_r,
+            device_id=at(x, y, z, 1 - c), device_id_type=MESH,
+        )
+
+    for d in range(1, ny):
+        qy_copy(lax.rem(y + d, ny)).start()
+    qbuf[x, y, c] = turned[...]
     acc[...] = jnp.full(acc.shape, BIG, jnp.float32)
 
     def g_copy(g, j):
         return pltpu.make_async_remote_copy(
             src_ref=gsrc.at[pl.ds(g * group, group), j],
             dst_ref=gbuf.at[me_yc, pl.ds(g * group, group)],
-            send_sem=g_s.at[g, j], recv_sem=g_r.at[g, me_yc],
-            device_id=at(x, lax.div(j, CORES), z, lax.rem(j, CORES)), device_id_type=MESH,
-        )
-
-    def g_got(g, j):
-        return pltpu.make_async_remote_copy(
-            src_ref=gsrc.at[pl.ds(g * group, group), j],
-            dst_ref=gbuf.at[j, pl.ds(g * group, group)],
-            send_sem=g_s.at[g, j], recv_sem=g_r.at[g, j],
+            send_sem=g_s, recv_sem=g_r,
             device_id=at(x, lax.div(j, CORES), z, lax.rem(j, CORES)), device_id_type=MESH,
         )
 
@@ -220,14 +214,10 @@
     origin = jnp.where(spare <= 0, tile * (USED - 1) + DEAD_SLOT + spare, jnp.where(spare == 1, tile + nyc * (USED - 1), -1))
     spread = onehot(lax.broadcasted_iota(jnp.int32, (nyc * TILE, block), 1) == origin)
 
-    @pl.loop(0, 4)
-    def _(g):
-        @pl.loop(g * group, jnp.minimum((g + 1) * group, nz - 1))
-        def _(k):
-            z_copy(k).wait_recv()
-
-        for i in range(group):
-            k = g * group + i
+    for g in range(4):
+        here = pl.ds(g * group, min(group, nz - 1 - g * group))
+        sent(zbuf.at[here], z_r.at[g])
+        for k in range(g * group, (g + 1) * group):
             tiles = jnp.dot(spread, zbuf[k], preferred_element_type=jnp.float32)
             gsrc[k] = tiles.astype(jnp.bfloat16).reshape(nyc, TILE, 128)
 
@@ -236,51 +226,30 @@
             g_copy(g, lax.rem(me_yc + d, nyc)).start()
 
         gbuf[me_yc, pl.ds(g * group, group)] = gsrc[pl.ds(g * group, group), me_yc]
-
-    def f_copy(i):
-        return pltpu.make_async_remote_copy(
-            src_ref=qbuf.at[xy_slot(i)], dst_ref=qbuf.at[xy_slot(i)], send_sem=f_s.at[i], recv_sem=f_r.at[i],
-            device_id=at(x, y, z, 1 - c), device_id_type=MESH,
-        )
-
-    def f_got(i):
-        other = i * CORES + 1 - c
-        return pltpu.make_async_remote_copy(
-            src_ref=qbuf.at[other], dst_ref=qbuf.at[other], send_sem=f_s.at[i], recv_sem=f_r.at[i],
-            device_id=at(x, y, z, 1 - c), device_id_type=MESH,
-        )
-
-    f_copy(me_xy).start()
-
-    @pl.loop(1, spots)
-    def _(d):
-        i = lax.rem(me_xy + d, spots)
-        q_copy(i, xy_slot(i)).wait_recv()
-        f_copy(i).start()
-
-    @pl.loop(0, 4)
-    def _(g):
-        @pl.loop(1, nyc)
-        def _(d):
-            g_got(g, lax.rem(me_yc + d, nyc)).wait_recv()
+        if g == 1:
+            sent(qbuf.at[0, 0 : ny - 1, 0], qy_r)
+            for d in range(1, nx):
+                qx_copy(lax.rem(x + d, nx)).start()
+
+    sent(gbuf.at[0 : nyc - 1], g_r)
 
     total = nyc * nz * TILE
     got = gbuf[...].reshape(total, 128)
+    got = jnp.concatenate([got, jnp.ones((total, 128), jnp.bfloat16)], axis=1)
     in_tile = lax.broadcasted_iota(jnp.int32, (8, 128), 1) & (TILE - 1)
     read = onehot(in_tile > DEAD_SLOT)
     tags = jnp.concatenate(
         [
-            jnp.dot(read, got[i * 128 : (i + 1) * 128], preferred_element_type=jnp.float32)[0:1]
+            jnp.dot(read, got[i * 128 : (i + 1) * 128, :128], preferred_element_type=jnp.float32)[0:1]
             for i in range(total // 128)
         ],
         axis=1,
     )
-    ones = jnp.ones((total, 128), jnp.bfloat16)
     name = (lax.broadcasted_iota(jnp.int32, (sub, total), 0) + 128).astype(jnp.float32)
 
     def x_copy(to, frm):
         return pltpu.make_async_remote_copy(
-            src_ref=rs_send.at[to], dst_ref=rs_recv.at[frm], send_sem=x_s.at[to], recv_sem=x_r.at[frm],
+            src_ref=rs_send.at[to], dst_ref=rs_recv.at[frm], send_sem=x_s, recv_sem=x_r,
             device_id=at(to, y, z, c), device_id_type=MESH,
         )
 
@@ -290,8 +259,8 @@
             scale = jnp.where(to == i, 0.5**i, scale)
         here = tags * scale
         hits = jnp.concatenate([onehot(name == here), onehot(name == here * 0.5**nx)], axis=0)
-        sums = jnp.dot(hits, got, preferred_element_type=jnp.float32)
-        count = jnp.dot(hits, ones, preferred_element_type=jnp.float32)
+        both = jnp.dot(hits, got, preferred_element_type=jnp.float32)
+        sums, count = both[:, :128], both[:, 128:]
         is_dead = count[sub:] > 0.5
         return jnp.where(is_dead, sums[sub:], sums[:sub]), jnp.where(is_dead, -1.0, count[:sub])
 
@@ -303,8 +272,10 @@
         ref[to, sub : sub + 8, :] = count.T[0:8]
         if d < nx:
             x_copy(to, x).start()
-    for d in range(1, nx):
-        x_copy(lax.rem(x + d, nx), lax.rem(x + d, nx)).wait_recv()
+
+    sent(qbuf.at[0 : nx - 1, :, 0], qx_r)
+    f_copy().start()
+    sent(rs_recv.at[0 : nx - 1], x_r)
 
     count = jnp.zeros((1, 128), jnp.float32)
     dead_row = jnp.zeros((1, 128), jnp.float32)
@@ -329,13 +300,13 @@
     def right(t):
         return pltpu.make_async_remote_copy(
             src_ref=code.at[jnp.maximum(2 * t - 1, 0)], dst_ref=code.at[2 * t + 1],
-            send_sem=right_s.at[t], recv_sem=right_r.at[t], device_id=along_z(1), device_id_type=MESH,
+            send_sem=right_s, recv_sem=right_r.at[t], device_id=along_z(1), device_id_type=MESH,
         )
 
     def left(t):
         return pltpu.make_async_remote_copy(
             src_ref=code.at[2 * t], dst_ref=code.at[2 * t + 2],
-            send_sem=left_s.at[t], recv_sem=left_r.at[t], device_id=along_z(-1), device_id_type=MESH,
+            send_sem=left_s, recv_sem=left_r.at[t], device_id=along_z(-1), device_id_type=MESH,
         )
 
     right(jnp.int32(0)).start()
@@ -347,13 +318,13 @@
     def b_copy(to, frm):
         span = pl.ds(pl.multiple_of(frm * sub, sub), sub)
         return pltpu.make_async_remote_copy(
-            src_ref=book.at[span], dst_ref=book.at[span], send_sem=b_s.at[to], recv_sem=b_r.at[frm],
+            src_ref=book.at[span], dst_ref=book.at[span], send_sem=b_s, recv_sem=b_r,
             device_id=at(to, y, z, c), device_id_type=MESH,
         )
 
     def c_copy(to, frm):
         return pltpu.make_async_remote_copy(
-            src_ref=cnts.at[frm], dst_ref=cnts.at[frm], send_sem=c_s.at[to], recv_sem=c_r.at[frm],
+            src_ref=cnts.at[frm], dst_ref=cnts.at[frm], send_sem=c_s, recv_sem=c_r,
             device_id=at(to, y, z, c), device_id_type=MESH,
         )
 
@@ -362,13 +333,11 @@
         b_copy(to, x).start()
         c_copy(to, x).start()
 
-    @pl.loop(0, spots)
-    def _(i):
-        f_got(i).wait_recv()
+    sent(qbuf.at[:, :, 0], f_r)
 
     def m_copy(to, frm):
         return pltpu.make_async_remote_copy(
-            src_ref=low_send.at[to], dst_ref=low_recv.at[frm], send_sem=m_s.at[to], recv_sem=m_r.at[frm],
+            src_ref=low_send.at[to], dst_ref=low_recv.at[frm], send_sem=m_s, recv_sem=m_r,
             device_id=in_plane(to), device_id_type=MESH,
         )
 
@@ -403,7 +372,7 @@
             for i in range(unroll):
                 p = lax.rem(me_p + 1 + o * unroll + i, planes)
                 score = jnp.dot(
-                    code[pl.ds(2 * t, 2)].reshape(2 * sub, 128), qbuf[p], preferred_element_type=jnp.float32
+                    code[pl.ds(2 * t, 2)].reshape(2 * sub, 128), qbuf[lax.div(p, nyc), lax.rem(lax.div(p, CORES), ny), lax.rem(p, CORES)], preferred_element_type=jnp.float32
                 )
                 lows = [
                     jnp.min((norm[...] + score[:, h * 128 : (h + 1) * 128]).reshape(2 * sub // 8, 8, 128), axis=0)
@@ -421,70 +390,30 @@
 
     low_recv[me_p] = lowest(me_p)
 
-    @pl.loop(1, planes)
-    def _(d):
-        frm = lax.rem(me_p + d, planes)
-        m_copy(frm, frm).wait_recv()
+    sent(low_recv.at[0 : planes - 1], m_r)
 
     best = jnp.min(low_recv[...], axis=0)
     for h in range(halves):
         first = h * (8 // halves)
         dist[h : h + 1, :] = (best[first : first + 1] + query_norm[:, h * 128 : (h + 1) * 128]) / 128
 
-    for d in range(1, nx):
-        frm = lax.rem(x + d, nx)
-        b_copy(frm, frm).wait_recv()
-        c_copy(frm, frm).wait_recv()
+    sent(book.at[0 : (nx - 1) * sub], b_r)
+    sent(cnts.at[0 : nx - 1], c_r)
     for i in range(nx):
         cnt_out[i : i + 1, :] = cnts[i, 0:1, :]
 
-    relay_in().wait_send()
-    relay_out().wait_send()
-
-    @pl.loop(1, nz - 1)
-    def _(k):
-        z_copy(k).wait_send()
-
-    @pl.loop(1, spots)
-    def _(d):
-        q_send(lax.rem(me_xy + d, spots)).wait_send()
-
-    @pl.loop(0, spots)
-    def _(i):
-        f_copy(i).wait_send()
-
-    @pl.loop(0, 4)
-    def _(g):
-        @pl.loop(1, nyc)
-        def _(d):
-            g_copy(g, lax.rem(me_yc + d, nyc)).wait_send()
-
-    for d in range(1, nx):
-        to = lax.rem(x + d, nx)
-        x_copy(to, x).wait_send()
-        b_copy(to, x).wait_send()
-        c_copy(to, x).wait_send()
-
-    @pl.loop(0, steps)
-    def _(t):
-        right(t).wait_send()
-
-        @pl.when(t < steps - 1)
-        def _():
-            left(t).wait_send()
-
-    @pl.loop(1, planes)
-    def _(d):
-        m_copy(lax.rem(me_p + d, planes), me_p).wait_send()
-
-
-def hand_over(book, counts, dist, book_out, counts_out, dist_out, sem):
-    pairs = ((book, book_out), (counts, counts_out), (dist, dist_out))
-    copies = [pltpu.make_async_copy(src, dst, sem.at[i]) for i, (src, dst) in enumerate(pairs)]
-    for copy in copies:
-        copy.start()
-    for copy in copies:
-        copy.wait()
+    sent(pack.at[0 : nz - 1], z_s)
+    sent(relay, relay_s)
+    sent(qbuf.at[0, 0 : ny - 1, 0], qy_s)
+    sent(qbuf.at[0 : nx - 1, :, 0], qx_s)
+    sent(qbuf.at[:, :, 0], f_s)
+    sent(gsrc.at[:, 0 : nyc - 1], g_s)
+    sent(rs_send.at[0 : nx - 1], x_s)
+    sent(book.at[0 : (nx - 1) * sub], b_s)
+    sent(cnts.at[0 : nx - 1], c_s)
+    sent(code.at[0:steps], right_s)
+    sent(code.at[0 : steps - 1], left_s)
+    sent(low_send.at[0 : planes - 1], m_s)
 
 
 def per_device(nx, ny, nz, latents, code_ids, ema_sums, ema_counts, dead_codes, restart_index, next_latents):
@@ -520,7 +449,7 @@
             pltpu.VMEM((nyc * USED, 128), bf16),
             pltpu.VMEM((nz, nyc, TILE, 128), bf16),
             pltpu.VMEM((nyc, nz, TILE, 128), bf16),
-            pltpu.VMEM((planes, 128, queries), bf16),
+            pltpu.VMEM((nx, ny, CORES, 128, queries), bf16),
             pltpu.VMEM((8, 128), jnp.int32),
             pltpu.VMEM((nx, sub + 8, 128), f32),
             pltpu.VMEM((nx, sub + 8, 128), f32),
@@ -531,17 +460,12 @@
             pltpu.VMEM((planes, 8, 128), f32),
             pltpu.VMEM((nx, 8, 128), f32),
             dma((7,)),
-            dma((nz,)), dma((nz,)),
+            dma, dma((4,)), dma, dma,
             dma, dma,
-            dma((4, nyc)), dma((4, nyc)),
-            dma((nx * ny,)), dma((nx * ny,)),
-            dma((nx * ny,)), dma((nx * ny,)),
-            dma((nx,)), dma((nx,)),
-            dma((nx,)), dma((nx,)),
-            dma((nx,)), dma((nx,)),
-            dma((nz // 2,)), dma((nz // 2,)),
-            dma((nz // 2,)), dma((nz // 2,)),
-            dma((planes,)), dma((planes,)),
+            dma, dma, dma, dma, dma, dma,
+            dma, dma, dma, dma, dma, dma,
+            dma, dma((nz // 2,)), dma, dma((nz // 2,)),
+            dma, dma,
         ],
         compiler_params=pltpu.CompilerParams(
             collective_id=0, has_side_effects=True, vmem_limit_bytes=56 * 1024 * 1024
@@ -550,18 +474,7 @@
         latents, code_ids.reshape(1, -1), dead_codes.reshape(1, -1), restart_index.reshape(1, -1),
         ema_sums, ema_counts.reshape(nx, sub), next_latents,
     )
-    return pl.pallas_call(
-        hand_over,
-        out_shape=(
-            jax.ShapeDtypeStruct((k_dev, 128), f32),
-            jax.ShapeDtypeStruct((k_dev,), f32),
-            jax.ShapeDtypeStruct((queries,), f32),
-        ),
-        in_specs=[hbm] * 3,
-        out_specs=(hbm,) * 3,
-        scratch_shapes=[dma((3,))],
-        compiler_params=pltpu.CompilerParams(vmem_limit_bytes=56 * 1024 * 1024),
-    )(book, counts.reshape(-1), dist.reshape(-1))
+    return book, counts.reshape(-1), dist.reshape(-1)
 
 
 def solution(mesh, ny=4):

time: 100 us -> 91.3 us (0.913)
  Pallas kernels: 99.7 us -> 87.5 us
  local copies, waits for them, and re-layouts: 0 us -> 2.91 us
    pallas_call x1 -> x0, Pallas kernels: 9.16 us -> none  [per_device(): pl.pallas_call(hand_over, out_shape=(jax.ShapeDtypeStruct((k_dev, 128), f...]
    pallas_call x1, Pallas kernels: 90.5 us -> 87.5 us  [per_device(): pl.pallas_call(functools.partial(body, nx, ny, nz), out_shape=(jax.ShapeD...]
    unnamed x0 -> x7, local copies, waits for them, and re-layouts: none -> 2.91 us
where the time goes in v4:
time: 91.3 us; the launch traced here: 91.1 us
  Pallas kernels  87.5 us (96%)
  local copies, waits for them, and re-layouts  2.91 us (3%)
    pallas_call x1, Pallas kernels, per_device(): pl.pallas_call(functools.partial(body, nx, ny, nz), out_shape=(jax.ShapeD...  87.5 us
    unnamed x7, local copies, waits for them, and re-layouts  2.91 us

profile of v4, /device:TPU:1, one launch (start us, length us, event | category | flops | bytes accessed | tf_op | source)
XLA Modules:
  0.0 91.1 jit_solution(10969868915129343281)
XLA Ops:
  0.6 87.5 %shard_map.94 = (f32[512,128]{1,0:T(8,128)}, f32[4,128]{1,0:T(4,128)}, f32[2,128]{1,0:T(2,128)}) custom-call(bf16[512,128]{1,0:T(8,128)(2,1)} %lat_in.1, s32[1,512]{1,0:T(1,128)} %bitcast.6, s32[1,32]{1,0:T(1,128)} %bitcast.10, s32[1,32]{1,0:T(1,128)} %bitcast.11, f32[512,128]{1,0:T(8,128)} %ema_s_in.1, f32[4,128]{1,0:T(4,128)} %bitcast.7, ...), custom_call_target="tpu_custom_call" | custom-call | tf_op jit(solution)/shard_map/pallas_call | solution.py:429
  88.2 0.0 copy-start
  88.2 1.7 %copy.13 = f32[512,128]{1,0:T(8,128)} copy(f32[512,128]{1,0:T(8,128)} %get-tuple-element.12) | data formatting | bytes 524288
  89.9 0.0 copy-done
  89.9 0.0 copy-start.1
  89.9 0.6 copy.14
  90.4 0.1 copy-done.1
  90.5 0.6 copy.15
Async XLA Ops:
  88.2 1.7 %copy-start = (f32[4,128]{1,0:T(4,128)S(1)}, f32[4,128]{1,0:T(4,128)}, u32[]{:S(2)}) copy-start(f32[4,128]{1,0:T(4,128)} %get-tuple-element.7) | copy-start | bytes 6148
  89.9 0.7 copy-start.1

commit v5 on v4

--- a/solution.py
+++ b/solution.py
@@ -27,7 +27,7 @@
 def body(
     nx, ny, nz, lat_in, ids_in, dead_in, ridx_in, ema_s_in, ema_c_in, nxt_in, book, cnt_out, dist,
     lat, ids, dead, ridx, ema_s, ema_c, nxt, turned,
-    pack, zbuf, relay, gsrc, gbuf, qbuf, ext, rs_send, rs_recv, code, norm, acc, low_send, low_recv, cnts, in_s,
+    pack, zbuf, relay, gsrc, gbuf, qbuf, ext, parts, rs_send, rs_recv, code, norm, acc, low_send, low_recv, cnts, in_s,
     z_s, z_r, relay_s, relay_r, g_s, g_r, qy_s, qy_r, qx_s, qx_r, f_s, f_r, x_s, x_r, b_s, b_r, c_s, c_r,
     right_s, right_r, left_s, left_r, m_s, m_r,
 ):
@@ -132,7 +132,7 @@
         to = goal == lax.rem(z + offset(k), nz)
         put = jnp.where(line == jnp.where(to, key, -1), 1.0, jnp.where(line == jnp.where(to, tag_key, -1), tag, 0.0))
         moved = jnp.dot(put.astype(jnp.bfloat16), data, preferred_element_type=jnp.float32)
-        here = lax.rem(me_yc * nz + k, 8)
+        here = lax.rem(me_yc * group + lax.rem(k, group), 8)
         tags = jnp.where(lane_tile == here, moved[:, 128:], 0.0)
         is_tag = lax.broadcasted_iota(jnp.int32, (block, 128), 0) >= nyc * (USED - 1)
         return jnp.where(is_tag, tags, moved[:, :128]).astype(jnp.bfloat16)
@@ -205,7 +205,7 @@
         return pltpu.make_async_remote_copy(
             src_ref=gsrc.at[pl.ds(g * group, group), j],
             dst_ref=gbuf.at[me_yc, pl.ds(g * group, group)],
-            send_sem=g_s, recv_sem=g_r,
+            send_sem=g_s, recv_sem=g_r.at[g],
             device_id=at(x, lax.div(j, CORES), z, lax.rem(j, CORES)), device_id_type=MESH,
         )
 
@@ -213,6 +213,25 @@
     tile, spare = row >> 4, (row & (TILE - 1)) - DEAD_SLOT
     origin = jnp.where(spare <= 0, tile * (USED - 1) + DEAD_SLOT + spare, jnp.where(spare == 1, tile + nyc * (USED - 1), -1))
     spread = onehot(lax.broadcasted_iota(jnp.int32, (nyc * TILE, block), 1) == origin)
+
+    total = nyc * group * TILE
+    in_tile = lax.broadcasted_iota(jnp.int32, (8, 128), 1) & (TILE - 1)
+    read = onehot(in_tile > DEAD_SLOT)
+    name = (lax.broadcasted_iota(jnp.int32, (sub, total), 0) + 128).astype(jnp.float32)
+
+    def arrived(g):
+        sent(gbuf.at[0 : nyc - 1, pl.ds(g * group, group)], g_r.at[g])
+        got = gbuf[:, pl.ds(g * group, group)].reshape(total, 128)
+        tags = [
+            jnp.dot(read, got[i * 128 : (i + 1) * 128], preferred_element_type=jnp.float32)[0:1]
+            for i in range(total // 128)
+        ]
+        return jnp.concatenate(tags, axis=1), jnp.concatenate([got, jnp.ones((total, 128), jnp.bfloat16)], axis=1)
+
+    def tally(tags, got, scale):
+        here = tags * scale
+        hits = jnp.concatenate([onehot(name == here), onehot(name == here * 0.5**nx)], axis=0)
+        return jnp.dot(hits, got, preferred_element_type=jnp.float32)
 
     for g in range(4):
         here = pl.ds(g * group, min(group, nz - 1 - g * group))
@@ -226,50 +245,34 @@
             g_copy(g, lax.rem(me_yc + d, nyc)).start()
 
         gbuf[me_yc, pl.ds(g * group, group)] = gsrc[pl.ds(g * group, group), me_yc]
+        if g > 0:
+            tags, got = arrived(g - 1)
+            for i in range(nx):
+                part = tally(tags, got, 0.5**i)
+                parts[i] = part if g == 1 else parts[i] + part
         if g == 1:
             sent(qbuf.at[0, 0 : ny - 1, 0], qy_r)
             for d in range(1, nx):
                 qx_copy(lax.rem(x + d, nx)).start()
 
-    sent(gbuf.at[0 : nyc - 1], g_r)
-
-    total = nyc * nz * TILE
-    got = gbuf[...].reshape(total, 128)
-    got = jnp.concatenate([got, jnp.ones((total, 128), jnp.bfloat16)], axis=1)
-    in_tile = lax.broadcasted_iota(jnp.int32, (8, 128), 1) & (TILE - 1)
-    read = onehot(in_tile > DEAD_SLOT)
-    tags = jnp.concatenate(
-        [
-            jnp.dot(read, got[i * 128 : (i + 1) * 128, :128], preferred_element_type=jnp.float32)[0:1]
-            for i in range(total // 128)
-        ],
-        axis=1,
-    )
-    name = (lax.broadcasted_iota(jnp.int32, (sub, total), 0) + 128).astype(jnp.float32)
-
     def x_copy(to, frm):
         return pltpu.make_async_remote_copy(
             src_ref=rs_send.at[to], dst_ref=rs_recv.at[frm], send_sem=x_s, recv_sem=x_r,
             device_id=at(to, y, z, c), device_id_type=MESH,
         )
 
-    def tally(to):
+    tags, got = arrived(3)
+    for d in range(1, nx + 1):
+        to = lax.rem(x + d, nx)
         scale = jnp.float32(1.0)
         for i in range(1, nx):
             scale = jnp.where(to == i, 0.5**i, scale)
-        here = tags * scale
-        hits = jnp.concatenate([onehot(name == here), onehot(name == here * 0.5**nx)], axis=0)
-        both = jnp.dot(hits, got, preferred_element_type=jnp.float32)
+        both = parts[to] + tally(tags, got, scale)
         sums, count = both[:, :128], both[:, 128:]
         is_dead = count[sub:] > 0.5
-        return jnp.where(is_dead, sums[sub:], sums[:sub]), jnp.where(is_dead, -1.0, count[:sub])
-
-    for d in range(1, nx + 1):
-        to = lax.rem(x + d, nx)
-        sums, count = tally(to)
         ref = rs_send if d < nx else rs_recv
-        ref[to, 0:sub, :] = sums
-        ref[to, sub : sub + 8, :] = count.T[0:8]
+        ref[to, 0:sub, :] = jnp.where(is_dead, sums[sub:], sums[:sub])
+        ref[to, sub : sub + 8, :] = jnp.where(is_dead, -1.0, count[:sub]).T[0:8]
         if d < nx:
             x_copy(to, x).start()
 
@@ -297,20 +300,24 @@
     rows_out = fresh / column(fresh_row)
     code[0] = (-2.0 * rows_out.astype(jnp.bfloat16).astype(jnp.float32)).astype(jnp.bfloat16)
 
-    def right(t):
-        return pltpu.make_async_remote_copy(
-            src_ref=code.at[jnp.maximum(2 * t - 1, 0)], dst_ref=code.at[2 * t + 1],
-            send_sem=right_s, recv_sem=right_r.at[t], device_id=along_z(1), device_id_type=MESH,
-        )
-
-    def left(t):
-        return pltpu.make_async_remote_copy(
-            src_ref=code.at[2 * t], dst_ref=code.at[2 * t + 2],
-            send_sem=left_s, recv_sem=left_r.at[t], device_id=along_z(-1), device_id_type=MESH,
-        )
-
-    right(jnp.int32(0)).start()
-    left(jnp.int32(0)).start()
+    rounds = nz // 4
+
+    def right(r, j):
+        return pltpu.make_async_remote_copy(
+            src_ref=code.at[jnp.maximum(4 * r - 2, 0)], dst_ref=code.at[4 * r + j],
+            send_sem=right_s, recv_sem=right_r.at[r], device_id=along_z(j), device_id_type=MESH,
+        )
+
+    def left(r, j):
+        return pltpu.make_async_remote_copy(
+            src_ref=code.at[4 * r], dst_ref=code.at[4 * r + 2 + j],
+            send_sem=left_s, recv_sem=left_r.at[r], device_id=along_z(-j), device_id_type=MESH,
+        )
+
+    right(jnp.int32(0), 2).start()
+    left(jnp.int32(0), 2).start()
+    right(jnp.int32(0), 1).start()
+    left(jnp.int32(0), 1).start()
 
     book[mine, :] = rows_out
     cnts[x] = jnp.broadcast_to(fresh_row, (8, 128))
@@ -348,39 +355,50 @@
         parts = [jnp.broadcast_to(small[:, h * 128 : (h + 1) * 128], (8 // halves, 128)) for h in range(halves)]
         return jnp.concatenate(parts, axis=0)
 
-    steps = nz // 2
-    unroll = min(16, planes // 2)
-
-    @pl.loop(0, steps)
+    unroll = min(8, planes // 2)
+    deep = 4 * sub
+
+    @pl.loop(0, rounds)
     def _(t):
-        right(t).wait_recv()
-
-        @pl.when(t < steps - 1)
+        sent(code.at[0:2], right_r.at[t])
+
+        @pl.when(t < rounds - 1)
         def _():
-            right(t + 1).start()
-            left(t).wait_recv()
-
-        @pl.when(t < steps - 2)
+            right(t + 1, 2).start()
+            sent(code.at[0:2], left_r.at[t])
+
+        @pl.when(t < rounds - 2)
         def _():
-            left(t + 1).start()
-
-        wide_table = code[pl.ds(2 * t, 2)].reshape(2 * sub, 128).astype(jnp.float32)
-        norm[...] = jnp.broadcast_to(0.25 * jnp.sum(wide_table * wide_table, axis=1, keepdims=True), (2 * sub, 128))
+            left(t + 1, 2).start()
+
+        @pl.when(t < rounds - 1)
+        def _():
+            right(t + 1, 1).start()
+            left(t + 1, 1).start()
+
+        @pl.when(t == rounds - 1)
+        def _():
+            sent(code.at[0], left_r.at[t])
+
+        wide_table = code[pl.ds(4 * t, 4)].reshape(deep, 128).astype(jnp.float32)
+        norm[...] = jnp.broadcast_to(0.25 * jnp.sum(wide_table * wide_table, axis=1, keepdims=True), (deep, 128))
 
         @pl.loop(0, planes // unroll)
         def _(o):
             for i in range(unroll):
                 p = lax.rem(me_p + 1 + o * unroll + i, planes)
                 score = jnp.dot(
-                    code[pl.ds(2 * t, 2)].reshape(2 * sub, 128), qbuf[lax.div(p, nyc), lax.rem(lax.div(p, CORES), ny), lax.rem(p, CORES)], preferred_element_type=jnp.float32
+                    code[pl.ds(4 * t, 4)].reshape(deep, 128),
+                    qbuf[lax.div(p, nyc), lax.rem(lax.div(p, CORES), ny), lax.rem(p, CORES)],
+                    preferred_element_type=jnp.float32,
                 )
                 lows = [
-                    jnp.min((norm[...] + score[:, h * 128 : (h + 1) * 128]).reshape(2 * sub // 8, 8, 128), axis=0)
+                    jnp.min((norm[...] + score[:, h * 128 : (h + 1) * 128]).reshape(deep // 8, 8, 128), axis=0)
                     for h in range(halves)
                 ]
                 acc[p] = jnp.minimum(acc[p], jnp.concatenate(lows, axis=1))
 
-            @pl.when(t == steps - 1)
+            @pl.when(t == rounds - 1)
             def _():
                 @pl.loop(o * unroll, jnp.minimum((o + 1) * unroll, planes - 1))
                 def _(i):
@@ -411,8 +429,8 @@
     sent(rs_send.at[0 : nx - 1], x_s)
     sent(book.at[0 : (nx - 1) * sub], b_s)
     sent(cnts.at[0 : nx - 1], c_s)
-    sent(code.at[0:steps], right_s)
-    sent(code.at[0 : steps - 1], left_s)
+    sent(code.at[0 : 2 * rounds], right_s)
+    sent(code.at[0 : 2 * rounds - 1], left_s)
     sent(low_send.at[0 : planes - 1], m_s)
 
 
@@ -451,20 +469,21 @@
             pltpu.VMEM((nyc, nz, TILE, 128), bf16),
             pltpu.VMEM((nx, ny, CORES, 128, queries), bf16),
             pltpu.VMEM((8, 128), jnp.int32),
+            pltpu.VMEM((nx, 2 * sub, 256), f32),
             pltpu.VMEM((nx, sub + 8, 128), f32),
             pltpu.VMEM((nx, sub + 8, 128), f32),
             pltpu.VMEM((nz, sub, 128), bf16),
-            pltpu.VMEM((2 * sub, 128), f32),
+            pltpu.VMEM((4 * sub, 128), f32),
             pltpu.VMEM((planes, 8, queries), f32),
             pltpu.VMEM((planes, 8, 128), f32),
             pltpu.VMEM((planes, 8, 128), f32),
             pltpu.VMEM((nx, 8, 128), f32),
             dma((7,)),
             dma, dma((4,)), dma, dma,
-            dma, dma,
+            dma, dma((4,)),
             dma, dma, dma, dma, dma, dma,
             dma, dma, dma, dma, dma, dma,
-            dma, dma((nz // 2,)), dma, dma((nz // 2,)),
+            dma, dma((nz // 4,)), dma, dma((nz // 4,)),
             dma, dma,
         ],
         compiler_params=pltpu.CompilerParams(

time: 91.3 us -> 90.5 us (level)
  no operation moved by 1% of the time
where the time goes in v5:
time: 90.5 us; the launch traced here: 90.4 us
  Pallas kernels  86.8 us (96%)
  local copies, waits for them, and re-layouts  2.91 us (3%)
    pallas_call x1, Pallas kernels, per_device(): pl.pallas_call(functools.partial(body, nx, ny, nz), out_shape=(jax.ShapeD...  86.8 us
    unnamed x7, local copies, waits for them, and re-layouts  2.91 us

profile of v5, /device:TPU:1, one launch (start us, length us, event | category | flops | bytes accessed | tf_op | source)
XLA Modules:
  0.0 90.4 jit_solution(10301602284356403647)
XLA Ops:
  0.6 86.8 %shard_map.94 = (f32[512,128]{1,0:T(8,128)}, f32[4,128]{1,0:T(4,128)}, f32[2,128]{1,0:T(2,128)}) custom-call(bf16[512,128]{1,0:T(8,128)(2,1)} %lat_in.1, s32[1,512]{1,0:T(1,128)} %bitcast.6, s32[1,32]{1,0:T(1,128)} %bitcast.10, s32[1,32]{1,0:T(1,128)} %bitcast.11, f32[512,128]{1,0:T(8,128)} %ema_s_in.1, f32[4,128]{1,0:T(4,128)} %bitcast.7, ...), custom_call_target="tpu_custom_call" | custom-call | tf_op jit(solution)/shard_map/pallas_call | solution.py:447
  87.5 0.0 copy-start
  87.5 1.7 %copy.13 = f32[512,128]{1,0:T(8,128)} copy(f32[512,128]{1,0:T(8,128)} %get-tuple-element.12) | data formatting | bytes 524288
  89.1 0.0 copy-done
  89.1 0.0 copy-start.1
  89.1 0.6 copy.14
  89.7 0.1 copy-done.1
  89.8 0.6 copy.15
Async XLA Ops:
  87.5 1.7 %copy-start = (f32[4,128]{1,0:T(4,128)S(1)}, f32[4,128]{1,0:T(4,128)}, u32[]{:S(2)}) copy-start(f32[4,128]{1,0:T(4,128)} %get-tuple-element.7) | copy-start | bytes 6148
  89.1 0.7 copy-start.1

commit v6 on v5

--- a/solution.py
+++ b/solution.py
@@ -24,15 +24,52 @@
     return jnp.broadcast_to(row, (128, 128)).T
 
 
-def body(
-    nx, ny, nz, lat_in, ids_in, dead_in, ridx_in, ema_s_in, ema_c_in, nxt_in, book, cnt_out, dist,
+def places(nx, ny, nz):
+    x = lax.axis_index("dp")
+    me = lax.axis_index("code")
+    c = lax.rem(me, CORES)
+    z = lax.rem(lax.div(me, CORES), nz)
+    y = lax.div(me, CORES * nz)
+    nyc = ny * CORES
+
+    def at(ax, ay, az, ac):
+        return (ax, (ay * nz + az) * CORES + ac)
+
+    def in_plane(p):
+        yc = lax.rem(p, nyc)
+        return at(lax.div(p, nyc), lax.div(yc, CORES), z, lax.rem(yc, CORES))
+
+    def along_z(d):
+        return at(x, y, lax.rem(z + d + nz, nz), c)
+
+    return x, y, z, c, at, in_plane, along_z
+
+
+def sent(ref, sem):
+    pltpu.make_async_copy(ref, ref, sem).wait()
+
+
+def meet(devices):
+    barrier = pltpu.get_barrier_semaphore()
+    count = 0
+    for first, last, where in devices:
+
+        @pl.loop(first, last)
+        def _(d, where=where):
+            pl.semaphore_signal(barrier, inc=1, device_id=where(d), device_id_type=MESH)
+
+        count += last - first
+    return lambda: pl.semaphore_wait(barrier, count)
+
+
+def update(
+    nx, ny, nz, lat_in, ids_in, dead_in, ridx_in, ema_s_in, ema_c_in, nxt_in, fresh_out, cnt_out, code_out, qnorm_out, qbuf,
     lat, ids, dead, ridx, ema_s, ema_c, nxt, turned,
-    pack, zbuf, relay, gsrc, gbuf, qbuf, ext, parts, rs_send, rs_recv, code, norm, acc, low_send, low_recv, cnts, in_s,
-    z_s, z_r, relay_s, relay_r, g_s, g_r, qy_s, qy_r, qx_s, qx_r, f_s, f_r, x_s, x_r, b_s, b_r, c_s, c_r,
-    right_s, right_r, left_s, left_r, m_s, m_r,
+    pack, zbuf, relay, gsrc, gbuf, ext, parts, rs_send, rs_recv, in_s,
+    z_s, z_r, relay_s, relay_r, g_s, g_r, qy_s, qy_r, qx_s, qx_r, f_s, f_r, x_s, x_r,
 ):
     rows = lat.shape[0]
-    k_dev = book.shape[0]
+    k_dev = ema_s_in.shape[0]
     sub = k_dev // nx
     queries = nxt.shape[0]
     nyc = ny * CORES
@@ -42,26 +79,9 @@
     shift_k = k_dev.bit_length() - 1
     shift_z = nz.bit_length() - 1
 
-    x = lax.axis_index("dp")
-    me = lax.axis_index("code")
-    c = lax.rem(me, CORES)
-    z = lax.rem(lax.div(me, CORES), nz)
-    y = lax.div(me, CORES * nz)
+    x, y, z, c, at, in_plane, along_z = places(nx, ny, nz)
     me_yc = y * CORES + c
     me_p = x * nyc + me_yc
-
-    def at(ax, ay, az, ac):
-        return (ax, (ay * nz + az) * CORES + ac)
-
-    def in_plane(p):
-        yc = lax.rem(p, nyc)
-        return at(lax.div(p, nyc), lax.div(yc, CORES), z, lax.rem(yc, CORES))
-
-    def sent(ref, sem):
-        pltpu.make_async_copy(ref, ref, sem).wait()
-
-    def along_z(d):
-        return at(x, y, lax.rem(z + d + nz, nz), c)
 
     mine = pl.ds(pl.multiple_of(x * sub, sub), sub)
     sources = (lat_in, ids_in, dead_in, ridx_in, nxt_in, ema_c_in, ema_s_in.at[mine])
@@ -72,15 +92,9 @@
     for load in loads:
         load.start()
 
-    barrier = pltpu.get_barrier_semaphore()
-
-    @pl.loop(1, planes)
-    def _(d):
-        pl.semaphore_signal(barrier, inc=1, device_id=in_plane(lax.rem(me_p + d, planes)), device_id_type=MESH)
-
-    @pl.loop(1, nz)
-    def _(d):
-        pl.semaphore_signal(barrier, inc=1, device_id=along_z(d), device_id_type=MESH)
+    met = meet(
+        [(1, planes, lambda d: in_plane(lax.rem(me_p + d, planes))), (1, nz, along_z)]
+    )
 
     for load in loads[:4]:
         load.wait()
@@ -156,7 +170,7 @@
         )
 
     pack[0] = packed(jnp.int32(0))
-    pl.semaphore_wait(barrier, planes - 1 + nz - 1)
+    met()
     relay_in().start()
 
     @pl.loop(0, half - 1)
@@ -199,7 +213,7 @@
     for d in range(1, ny):
         qy_copy(lax.rem(y + d, ny)).start()
     qbuf[x, y, c] = turned[...]
-    acc[...] = jnp.full(acc.shape, BIG, jnp.float32)
+    qnorm_out[...] = jnp.broadcast_to(query_norm, qnorm_out.shape)
 
     def g_copy(g, j):
         return pltpu.make_async_remote_copy(
@@ -298,7 +312,45 @@
     fresh = DECAY * ema_s[...] + (1.0 - DECAY) * sums
     fresh = jnp.where(column(dead_row) > 0.5, restart, fresh)
     rows_out = fresh / column(fresh_row)
-    code[0] = (-2.0 * rows_out.astype(jnp.bfloat16).astype(jnp.float32)).astype(jnp.bfloat16)
+    fresh_out[...] = rows_out
+    cnt_out[...] = jnp.broadcast_to(fresh_row, (8, 128))
+    code_out[...] = (-2.0 * rows_out.astype(jnp.bfloat16).astype(jnp.float32)).astype(jnp.bfloat16)
+
+    sent(qbuf.at[:, :, 0], f_r)
+
+    sent(pack.at[0 : nz - 1], z_s)
+    sent(relay, relay_s)
+    sent(qbuf.at[0, 0 : ny - 1, 0], qy_s)
+    sent(qbuf.at[0 : nx - 1, :, 0], qx_s)
+    sent(qbuf.at[:, :, 0], f_s)
+    sent(gsrc.at[:, 0 : nyc - 1], g_s)
+    sent(rs_send.at[0 : nx - 1], x_s)
+
+
+def nearest(
+    nx, ny, nz, rows_in, cnt_in, own, qnorm, qbuf, book, cnt_out, dist,
+    code, norm, acc, low_send, low_recv, cnts,
+    b_s, b_r, c_s, c_r, right_s, right_r, left_s, left_r, m_s, m_r,
+):
+    sub = own.shape[0]
+    nyc = ny * CORES
+    planes = nx * nyc
+    queries = qbuf.shape[-1]
+    x, y, z, c, at, in_plane, along_z = places(nx, ny, nz)
+    me_p = x * nyc + y * CORES + c
+    mine = pl.ds(pl.multiple_of(x * sub, sub), sub)
+    met = meet(
+        [
+            (1, planes, lambda d: in_plane(lax.rem(me_p + d, planes))),
+            (1, 3, along_z),
+            (1, 3, lambda d: along_z(-d)),
+        ]
+    )
+    code[0] = own[...]
+    acc[...] = jnp.full(acc.shape, BIG, jnp.float32)
+    book[mine, :] = rows_in[...]
+    cnts[x] = cnt_in[...]
+    met()
 
     rounds = nz // 4
 
@@ -319,9 +371,6 @@
     right(jnp.int32(0), 1).start()
     left(jnp.int32(0), 1).start()
 
-    book[mine, :] = rows_out
-    cnts[x] = jnp.broadcast_to(fresh_row, (8, 128))
-
     def b_copy(to, frm):
         span = pl.ds(pl.multiple_of(frm * sub, sub), sub)
         return pltpu.make_async_remote_copy(
@@ -339,8 +388,6 @@
         to = lax.rem(x + d, nx)
         b_copy(to, x).start()
         c_copy(to, x).start()
-
-    sent(qbuf.at[:, :, 0], f_r)
 
     def m_copy(to, frm):
         return pltpu.make_async_remote_copy(
@@ -413,20 +460,13 @@
     best = jnp.min(low_recv[...], axis=0)
     for h in range(halves):
         first = h * (8 // halves)
-        dist[h : h + 1, :] = (best[first : first + 1] + query_norm[:, h * 128 : (h + 1) * 128]) / 128
+        dist[h : h + 1, :] = (best[first : first + 1] + qnorm[0:1, h * 128 : (h + 1) * 128]) / 128
 
     sent(book.at[0 : (nx - 1) * sub], b_r)
     sent(cnts.at[0 : nx - 1], c_r)
     for i in range(nx):
         cnt_out[i : i + 1, :] = cnts[i, 0:1, :]
 
-    sent(pack.at[0 : nz - 1], z_s)
-    sent(relay, relay_s)
-    sent(qbuf.at[0, 0 : ny - 1, 0], qy_s)
-    sent(qbuf.at[0 : nx - 1, :, 0], qx_s)
-    sent(qbuf.at[:, :, 0], f_s)
-    sent(gsrc.at[:, 0 : nyc - 1], g_s)
-    sent(rs_send.at[0 : nx - 1], x_s)
     sent(book.at[0 : (nx - 1) * sub], b_s)
     sent(cnts.at[0 : nx - 1], c_s)
     sent(code.at[0 : 2 * rounds], right_s)
@@ -444,15 +484,18 @@
     vmem = pl.BlockSpec(memory_space=pltpu.VMEM)
     dma = pltpu.SemaphoreType.DMA
     bf16, f32 = jnp.bfloat16, jnp.float32
-    book, counts, dist = pl.pallas_call(
-        functools.partial(body, nx, ny, nz),
+    wide = pltpu.CompilerParams(collective_id=0, has_side_effects=True, vmem_limit_bytes=40 * 1024 * 1024)
+    rows_out, counts, own, qnorm, qbuf = pl.pallas_call(
+        functools.partial(update, nx, ny, nz),
         out_shape=(
-            jax.ShapeDtypeStruct((k_dev, 128), f32),
-            jax.ShapeDtypeStruct((nx, sub), f32),
-            jax.ShapeDtypeStruct((queries // 128, 128), f32),
+            jax.ShapeDtypeStruct((sub, 128), f32),
+            jax.ShapeDtypeStruct((8, sub), f32),
+            jax.ShapeDtypeStruct((sub, 128), bf16),
+            jax.ShapeDtypeStruct((8, queries), f32),
+            jax.ShapeDtypeStruct((nx, ny, CORES, 128, queries), bf16),
         ),
         in_specs=[hbm] * 7,
-        out_specs=(vmem,) * 3,
+        out_specs=(vmem,) * 5,
         scratch_shapes=[
             pltpu.VMEM(latents.shape, bf16),
             pltpu.VMEM((1, code_ids.shape[0]), jnp.int32),
@@ -467,32 +510,45 @@
             pltpu.VMEM((nyc * USED, 128), bf16),
             pltpu.VMEM((nz, nyc, TILE, 128), bf16),
             pltpu.VMEM((nyc, nz, TILE, 128), bf16),
-            pltpu.VMEM((nx, ny, CORES, 128, queries), bf16),
             pltpu.VMEM((8, 128), jnp.int32),
             pltpu.VMEM((nx, 2 * sub, 256), f32),
             pltpu.VMEM((nx, sub + 8, 128), f32),
             pltpu.VMEM((nx, sub + 8, 128), f32),
+            dma((7,)),
+            dma, dma((4,)), dma, dma,
+            dma, dma((4,)),
+            dma, dma, dma, dma, dma, dma,
+            dma, dma,
+        ],
+        compiler_params=wide,
+    )(
+        latents, code_ids.reshape(1, -1), dead_codes.reshape(1, -1), restart_index.reshape(1, -1),
+        ema_sums, ema_counts.reshape(nx, sub), next_latents,
+    )
+    book, counts, dist = pl.pallas_call(
+        functools.partial(nearest, nx, ny, nz),
+        out_shape=(
+            jax.ShapeDtypeStruct((k_dev, 128), f32),
+            jax.ShapeDtypeStruct((nx, sub), f32),
+            jax.ShapeDtypeStruct((queries // 128, 128), f32),
+        ),
+        in_specs=[vmem] * 5,
+        out_specs=(vmem,) * 3,
+        scratch_shapes=[
             pltpu.VMEM((nz, sub, 128), bf16),
             pltpu.VMEM((4 * sub, 128), f32),
             pltpu.VMEM((planes, 8, queries), f32),
             pltpu.VMEM((planes, 8, 128), f32),
             pltpu.VMEM((planes, 8, 128), f32),
             pltpu.VMEM((nx, 8, 128), f32),
-            dma((7,)),
-            dma, dma((4,)), dma, dma,
-            dma, dma((4,)),
-            dma, dma, dma, dma, dma, dma,
-            dma, dma, dma, dma, dma, dma,
+            dma, dma, dma, dma,
             dma, dma((nz // 4,)), dma, dma((nz // 4,)),
             dma, dma,
         ],
         compiler_params=pltpu.CompilerParams(
-            collective_id=0, has_side_effects=True, vmem_limit_bytes=56 * 1024 * 1024
+            collective_id=1, has_side_effects=True, vmem_limit_bytes=40 * 1024 * 1024
         ),
-    )(
-        latents, code_ids.reshape(1, -1), dead_codes.reshape(1, -1), restart_index.reshape(1, -1),
-        ema_sums, ema_counts.reshape(nx, sub), next_latents,
-    )
+    )(rows_out, counts, own, qnorm, qbuf)
     return book, counts.reshape(-1), dist.reshape(-1)
 
 

time: 90.5 us -> 98.8 us (1.092)
  local copies, waits for them, and re-layouts: 2.91 us -> 7.2 us
  Pallas kernels: 86.8 us -> 90.6 us
    unnamed x7 -> x17, local copies, waits for them, and re-layouts: 2.91 us -> 7.2 us
    pallas_call x1 -> x2, Pallas kernels: 86.8 us -> 90.6 us  [the longest x1 61.4 us: per_device(): pl.pallas_call(functools.partial(update, nx, ny, nz), out_shape=(jax.Shap...]
where the time goes in v6:
time: 98.8 us; the launch traced here: 98.5 us
  Pallas kernels  90.6 us (92%)
  local copies, waits for them, and re-layouts  7.2 us (7%)
    pallas_call x1, Pallas kernels, per_device(): pl.pallas_call(functools.partial(update, nx, ny, nz), out_shape=(jax.Shap...  61.4 us
    pallas_call x1, Pallas kernels, per_device(): pl.pallas_call(functools.partial(nearest, nx, ny, nz), out_shape=(jax.Sha...  29.2 us
    unnamed x17, local copies, waits for them, and re-layouts  7.2 us

profile of v6, /device:TPU:1, one launch (start us, length us, event | category | flops | bytes accessed | tf_op | source)
XLA Modules:
  0.0 98.5 jit_solution(4845102761216079628)
XLA Ops:
  0.6 0.0 copy-start
  0.6 0.9 copy-done
  1.6 0.0 copy-start.1
  1.6 0.9 copy-done.1
  2.5 0.0 copy-start.2
  2.5 0.8 copy-done.2
  3.3 0.0 copy-start.3
  3.3 0.7 copy-done.3
  4.0 0.0 copy-start.4
  4.0 0.7 copy-done.4
  4.7 0.0 copy-start.5
  4.7 0.7 copy-done.5
  5.3 0.0 copy-start.6
  5.4 0.7 copy-done.6
  6.0 61.4 %shard_map.94 = (f32[128,128]{1,0:T(8,128)S(1)}, f32[8,128]{1,0:T(8,128)S(1)}, bf16[128,128]{1,0:T(8,128)(2,1)S(1)}, f32[8,256]{1,0:T(8,128)S(1)}, bf16[4,4,2,128,256]{4,3,2,1,0:T(8,128)(2,1)S(1)}) custom-call(bf16[512,128]{1,0:T(8,128)(2,1)S(1)} %copy-done.1, s32[1,512]{1,0:T(1,128)S(1)} %bitcast.6, s32[1,32]{1,0:T(1,128)S(1)} %bitcast.10, ...), custom_call_target="tpu_custom_call" | custom-call | tf_op jit(solution)/shard_map/pallas_call | solution.py:488
  67.4 29.2 %shard_map.95 = (f32[512,128]{1,0:T(8,128)S(1)}, f32[4,128]{1,0:T(4,128)S(1)}, f32[2,128]{1,0:T(2,128)S(1)}) custom-call(f32[128,128]{1,0:T(8,128)S(1)} %get-tuple-element.11.rows_in, f32[8,128]{1,0:T(8,128)S(1)} %get-tuple-element.12.cnt_in, bf16[128,128]{1,0:T(8,128)(2,1)S(1)} %get-tuple-element.13.own, f32[8,256]{1,0:T(8,128)S(1)} %get-tuple-element.14.qnorm, ...), custom_call_target="tpu_custom_call" | custom-call | tf_op jit(solution)/shard_map/pallas_call | solution.py:528
  96.6 0.7 copy.13
  97.3 0.6 copy.14
  97.9 0.6 copy.15
Async XLA Ops:
  0.6 1.0 copy-start
  1.6 0.9 copy-start.1
  2.5 0.8 copy-start.2
  3.3 0.7 copy-start.3
  4.0 0.7 copy-start.4
  4.7 0.7 copy-start.5
  5.3 0.7 copy-start.6

commit v7 on v5

--- a/solution.py
+++ b/solution.py
@@ -28,7 +28,7 @@
     nx, ny, nz, lat_in, ids_in, dead_in, ridx_in, ema_s_in, ema_c_in, nxt_in, book, cnt_out, dist,
     lat, ids, dead, ridx, ema_s, ema_c, nxt, turned,
     pack, zbuf, relay, gsrc, gbuf, qbuf, ext, parts, rs_send, rs_recv, code, norm, acc, low_send, low_recv, cnts, in_s,
-    z_s, z_r, relay_s, relay_r, g_s, g_r, qy_s, qy_r, qx_s, qx_r, f_s, f_r, x_s, x_r, b_s, b_r, c_s, c_r,
+    z_s, z_r, relay_s, relay_r, g_s, g_r, q1_s, q1_r, q2_s, q2_r, q3_s, q3_r, f_s, f_r, x_s, x_r, b_s, b_r, c_s, c_r,
     right_s, right_r, left_s, left_r, m_s, m_r,
 ):
     rows = lat.shape[0]
@@ -155,9 +155,66 @@
             device_id=along_z(way * (half - 1)), device_id_type=MESH,
         )
 
+    def neighbour(axis, d):
+        if axis == "x":
+            return at(lax.rem(x + d + nx, nx), y, z, c)
+        return at(x, lax.rem(y + d + ny, ny), z, c)
+
+    def send(src, dst, sems, device):
+        return pltpu.make_async_remote_copy(
+            src_ref=src, dst_ref=dst, send_sem=sems[0], recv_sem=sems[1], device_id=device, device_id_type=MESH
+        )
+
+    one, two, three = (q1_s, q1_r), (q2_s, q2_r), (q3_s, q3_r)
+    cores = ((0, "y", "x"), (1, "x", "y"))
+
+    def queries_one():
+        for core, axis, _ in cores:
+
+            @pl.when(c == core)
+            def _(core=core, axis=axis):
+                for d in range(1, ny):
+                    send(turned, qbuf.at[x, y, core], one, neighbour(axis, d)).start()
+
+    def queries_two():
+        sent(qbuf.at[0, 0 : ny - 1, 0], q1_r)
+        for core, _, axis in cores:
+
+            @pl.when(c == core)
+            def _(core=core, axis=axis):
+                line_of = qbuf.at[x, :, core] if axis == "x" else qbuf.at[:, y, core]
+                send(line_of, line_of, two, neighbour(axis, 1)).start()
+                send(line_of, line_of, two, neighbour(axis, -1)).start()
+
+    def queries_three():
+        sent(qbuf.at[0:2, :, 0], q2_r)
+        for core, _, axis in cores:
+
+            @pl.when(c == core)
+            def _(core=core, axis=axis):
+                lower, upper = pl.ds(0, ny // 2), pl.ds(ny // 2, ny // 2)
+                if axis == "x":
+                    before, after = lax.rem(x + nx - 1, nx), lax.rem(x + 1, nx)
+                    on, back = qbuf.at[before, lower, core], qbuf.at[after, upper, core]
+                else:
+                    before, after = lax.rem(y + ny - 1, ny), lax.rem(y + 1, ny)
+                    on, back = qbuf.at[lower, before, core], qbuf.at[upper, after, core]
+                send(on, on, three, neighbour(axis, 1)).start()
+                send(back, back, three, neighbour(axis, -1)).start()
+
+    def queries_across():
+        mine_too = qbuf.at[:, :, c]
+        return send(mine_too, mine_too, (f_s, f_r), at(x, y, z, 1 - c))
+
+    loads[4].wait()
+    wide = nxt[...].astype(jnp.float32)
+    query_norm = jnp.sum((wide * wide).T, axis=0, keepdims=True)
+    turned[...] = wide.T.astype(jnp.bfloat16)
+    qbuf[x, y, c] = turned[...]
     pack[0] = packed(jnp.int32(0))
     pl.semaphore_wait(barrier, planes - 1 + nz - 1)
     relay_in().start()
+    queries_one()
 
     @pl.loop(0, half - 1)
     def _(o):
@@ -172,33 +229,8 @@
             relay_out().start()
 
     zbuf[nz - 1] = packed(jnp.int32(nz - 1))
-
-    loads[4].wait()
-    wide = nxt[...].astype(jnp.float32)
-    query_norm = jnp.sum((wide * wide).T, axis=0, keepdims=True)
-    turned[...] = wide.T.astype(jnp.bfloat16)
-
-    def qy_copy(to):
-        return pltpu.make_async_remote_copy(
-            src_ref=turned, dst_ref=qbuf.at[x, y, c], send_sem=qy_s, recv_sem=qy_r,
-            device_id=at(x, to, z, c), device_id_type=MESH,
-        )
-
-    def qx_copy(to):
-        return pltpu.make_async_remote_copy(
-            src_ref=qbuf.at[x, :, c], dst_ref=qbuf.at[x, :, c], send_sem=qx_s, recv_sem=qx_r,
-            device_id=at(to, y, z, c), device_id_type=MESH,
-        )
-
-    def f_copy():
-        return pltpu.make_async_remote_copy(
-            src_ref=qbuf.at[:, :, c], dst_ref=qbuf.at[:, :, c], send_sem=f_s, recv_sem=f_r,
-            device_id=at(x, y, z, 1 - c), device_id_type=MESH,
-        )
-
-    for d in range(1, ny):
-        qy_copy(lax.rem(y + d, ny)).start()
-    qbuf[x, y, c] = turned[...]
+    queries_two()
+
     acc[...] = jnp.full(acc.shape, BIG, jnp.float32)
 
     def g_copy(g, j):
@@ -250,10 +282,11 @@
             for i in range(nx):
                 part = tally(tags, got, 0.5**i)
                 parts[i] = part if g == 1 else parts[i] + part
+        if g == 0:
+            queries_three()
         if g == 1:
-            sent(qbuf.at[0, 0 : ny - 1, 0], qy_r)
-            for d in range(1, nx):
-                qx_copy(lax.rem(x + d, nx)).start()
+            sent(qbuf.at[0, :, 0], q3_r)
+            queries_across().start()
 
     def x_copy(to, frm):
         return pltpu.make_async_remote_copy(
@@ -276,8 +309,6 @@
         if d < nx:
             x_copy(to, x).start()
 
-    sent(qbuf.at[0 : nx - 1, :, 0], qx_r)
-    f_copy().start()
     sent(rs_recv.at[0 : nx - 1], x_r)
 
     count = jnp.zeros((1, 128), jnp.float32)
@@ -315,7 +346,8 @@
         )
 
     right(jnp.int32(0), 2).start()
-    left(jnp.int32(0), 2).start()
+    if rounds > 1:
+        left(jnp.int32(0), 2).start()
     right(jnp.int32(0), 1).start()
     left(jnp.int32(0), 1).start()
 
@@ -352,59 +384,70 @@
 
     def lowest(p):
         small = jnp.min(acc[p], axis=0, keepdims=True)
-        parts = [jnp.broadcast_to(small[:, h * 128 : (h + 1) * 128], (8 // halves, 128)) for h in range(halves)]
-        return jnp.concatenate(parts, axis=0)
+        parts_of = [jnp.broadcast_to(small[:, h * 128 : (h + 1) * 128], (8 // halves, 128)) for h in range(halves)]
+        return jnp.concatenate(parts_of, axis=0)
 
     unroll = min(8, planes // 2)
-    deep = 4 * sub
-
-    @pl.loop(0, rounds)
+    spread_out = planes // unroll
+
+    def norms(first, count):
+        table = code[pl.ds(first, count)].reshape(count * sub, 128).astype(jnp.float32)
+        both = 0.25 * jnp.sum(table * table, axis=1, keepdims=True)
+        norm[0 : count * sub] = jnp.broadcast_to(both, (count * sub, 128))
+
+    def compare(first, count, o):
+        deep = count * sub
+        for i in range(unroll):
+            p = lax.rem(me_p + 1 + o * unroll + i, planes)
+            score = jnp.dot(
+                code[pl.ds(first, count)].reshape(deep, 128),
+                qbuf[lax.div(p, nyc), lax.rem(lax.div(p, CORES), ny), lax.rem(p, CORES)],
+                preferred_element_type=jnp.float32,
+            )
+            lows = [
+                jnp.min((norm[0:deep] + score[:, h * 128 : (h + 1) * 128]).reshape(deep // 8, 8, 128), axis=0)
+                for h in range(halves)
+            ]
+            acc[p] = jnp.minimum(acc[p], jnp.concatenate(lows, axis=1))
+
+    norms(0, 1)
+
+    @pl.loop(0, spread_out)
+    def _(o):
+        compare(0, 1, o)
+
+    @pl.loop(0, rounds - 1)
     def _(t):
         sent(code.at[0:2], right_r.at[t])
-
-        @pl.when(t < rounds - 1)
-        def _():
-            right(t + 1, 2).start()
-            sent(code.at[0:2], left_r.at[t])
+        right(t + 1, 2).start()
+        sent(code.at[0:2], left_r.at[t])
 
         @pl.when(t < rounds - 2)
         def _():
             left(t + 1, 2).start()
 
-        @pl.when(t < rounds - 1)
-        def _():
-            right(t + 1, 1).start()
-            left(t + 1, 1).start()
-
-        @pl.when(t == rounds - 1)
-        def _():
-            sent(code.at[0], left_r.at[t])
-
-        wide_table = code[pl.ds(4 * t, 4)].reshape(deep, 128).astype(jnp.float32)
-        norm[...] = jnp.broadcast_to(0.25 * jnp.sum(wide_table * wide_table, axis=1, keepdims=True), (deep, 128))
-
-        @pl.loop(0, planes // unroll)
+        right(t + 1, 1).start()
+        left(t + 1, 1).start()
+        norms(4 * t + 1, 4)
+
+        @pl.loop(0, spread_out)
         def _(o):
-            for i in range(unroll):
-                p = lax.rem(me_p + 1 + o * unroll + i, planes)
-                score = jnp.dot(
-                    code[pl.ds(4 * t, 4)].reshape(deep, 128),
-                    qbuf[lax.div(p, nyc), lax.rem(lax.div(p, CORES), ny), lax.rem(p, CORES)],
-                    preferred_element_type=jnp.float32,
-                )
-                lows = [
-                    jnp.min((norm[...] + score[:, h * 128 : (h + 1) * 128]).reshape(deep // 8, 8, 128), axis=0)
-                    for h in range(halves)
-                ]
-                acc[p] = jnp.minimum(acc[p], jnp.concatenate(lows, axis=1))
-
-            @pl.when(t == rounds - 1)
-            def _():
-                @pl.loop(o * unroll, jnp.minimum((o + 1) * unroll, planes - 1))
-                def _(i):
-                    to = lax.rem(me_p + 1 + i, planes)
-                    low_send[to] = lowest(to)
-                    m_copy(to, me_p).start()
+            compare(4 * t + 1, 4, o)
+
+    last = 4 * (rounds - 1) + 1
+    sent(code.at[0:2], right_r.at[rounds - 1])
+    sent(code.at[0], left_r.at[rounds - 1])
+    norms(last, 3)
+
+    @pl.loop(0, spread_out)
+    def _(o):
+        compare(last, 3, o)
+
+        @pl.loop(o * unroll, jnp.minimum((o + 1) * unroll, planes - 1))
+        def _(i):
+            to = lax.rem(me_p + 1 + i, planes)
+            low_send[to] = lowest(to)
+            m_copy(to, me_p).start()
 
     low_recv[me_p] = lowest(me_p)
 
@@ -422,8 +465,9 @@
 
     sent(pack.at[0 : nz - 1], z_s)
     sent(relay, relay_s)
-    sent(qbuf.at[0, 0 : ny - 1, 0], qy_s)
-    sent(qbuf.at[0 : nx - 1, :, 0], qx_s)
+    sent(qbuf.at[0, 0 : ny - 1, 0], q1_s)
+    sent(qbuf.at[0:2, :, 0], q2_s)
+    sent(qbuf.at[0, :, 0], q3_s)
     sent(qbuf.at[:, :, 0], f_s)
     sent(gsrc.at[:, 0 : nyc - 1], g_s)
     sent(rs_send.at[0 : nx - 1], x_s)
@@ -481,7 +525,7 @@
             dma((7,)),
             dma, dma((4,)), dma, dma,
             dma, dma((4,)),
-            dma, dma, dma, dma, dma, dma,
+            dma, dma, dma, dma, dma, dma, dma, dma,
             dma, dma, dma, dma, dma, dma,
             dma, dma((nz // 4,)), dma, dma((nz // 4,)),
             dma, dma,

time: 90.5 us -> 84.5 us (0.934)
  Pallas kernels: 86.8 us -> 80.8 us
    pallas_call x1, Pallas kernels: 86.8 us -> 80.8 us  [per_device(): pl.pallas_call(functools.partial(body, nx, ny, nz), out_shape=(jax.ShapeD...]
where the time goes in v7:
time: 84.5 us; the launch traced here: 84.4 us
  Pallas kernels  80.8 us (96%)
  local copies, waits for them, and re-layouts  2.91 us (3%)
    pallas_call x1, Pallas kernels, per_device(): pl.pallas_call(functools.partial(body, nx, ny, nz), out_shape=(jax.ShapeD...  80.8 us
    unnamed x7, local copies, waits for them, and re-layouts  2.91 us

profile of v7, /device:TPU:1, one launch (start us, length us, event | category | flops | bytes accessed | tf_op | source)
XLA Modules:
  0.0 84.4 jit_solution(13707067687074608603)
XLA Ops:
  0.6 80.8 %shard_map.94 = (f32[512,128]{1,0:T(8,128)}, f32[4,128]{1,0:T(4,128)}, f32[2,128]{1,0:T(2,128)}) custom-call(bf16[512,128]{1,0:T(8,128)(2,1)} %lat_in.1, s32[1,512]{1,0:T(1,128)} %bitcast.6, s32[1,32]{1,0:T(1,128)} %bitcast.10, s32[1,32]{1,0:T(1,128)} %bitcast.11, f32[512,128]{1,0:T(8,128)} %ema_s_in.1, f32[4,128]{1,0:T(4,128)} %bitcast.7, ...), custom_call_target="tpu_custom_call" | custom-call | tf_op jit(solution)/shard_map/pallas_call | solution.py:491
  81.4 0.0 copy-start
  81.4 1.7 %copy.13 = f32[512,128]{1,0:T(8,128)} copy(f32[512,128]{1,0:T(8,128)} %get-tuple-element.12) | data formatting | bytes 524288
  83.1 0.0 copy-done
  83.1 0.0 copy-start.1
  83.1 0.6 copy.14
  83.7 0.1 copy-done.1
  83.8 0.6 copy.15
Async XLA Ops:
  81.4 1.7 %copy-start = (f32[4,128]{1,0:T(4,128)S(1)}, f32[4,128]{1,0:T(4,128)}, u32[]{:S(2)}) copy-start(f32[4,128]{1,0:T(4,128)} %get-tuple-element.7) | copy-start | bytes 6148
  83.1 0.7 copy-start.1

commit v8 on v7

--- a/solution.py
+++ b/solution.py
@@ -387,8 +387,10 @@
         parts_of = [jnp.broadcast_to(small[:, h * 128 : (h + 1) * 128], (8 // halves, 128)) for h in range(halves)]
         return jnp.concatenate(parts_of, axis=0)
 
-    unroll = min(8, planes // 2)
-    spread_out = planes // unroll
+    chips = nx * ny
+    me_chip = x * ny + y
+    unroll = 4
+    spread_out = chips // unroll
 
     def norms(first, count):
         table = code[pl.ds(first, count)].reshape(count * sub, 128).astype(jnp.float32)
@@ -398,17 +400,20 @@
     def compare(first, count, o):
         deep = count * sub
         for i in range(unroll):
-            p = lax.rem(me_p + 1 + o * unroll + i, planes)
+            chip = lax.rem(me_chip + 1 + o * unroll + i, chips)
+            px, py = lax.div(chip, ny), lax.rem(chip, ny)
             score = jnp.dot(
                 code[pl.ds(first, count)].reshape(deep, 128),
-                qbuf[lax.div(p, nyc), lax.rem(lax.div(p, CORES), ny), lax.rem(p, CORES)],
+                jnp.concatenate([qbuf[px, py, j] for j in range(CORES)], axis=1),
                 preferred_element_type=jnp.float32,
             )
             lows = [
                 jnp.min((norm[0:deep] + score[:, h * 128 : (h + 1) * 128]).reshape(deep // 8, 8, 128), axis=0)
-                for h in range(halves)
+                for h in range(CORES * halves)
             ]
-            acc[p] = jnp.minimum(acc[p], jnp.concatenate(lows, axis=1))
+            for j in range(CORES):
+                low = jnp.concatenate(lows[j * halves : (j + 1) * halves], axis=1)
+                acc[chip * CORES + j] = jnp.minimum(acc[chip * CORES + j], low)
 
     norms(0, 1)
 
@@ -443,9 +448,10 @@
     def _(o):
         compare(last, 3, o)
 
-        @pl.loop(o * unroll, jnp.minimum((o + 1) * unroll, planes - 1))
+        @pl.loop(o * unroll * CORES, jnp.minimum((o + 1) * unroll * CORES, planes - 1))
         def _(i):
-            to = lax.rem(me_p + 1 + i, planes)
+            chip = lax.rem(me_chip + 1 + lax.div(i, CORES), chips)
+            to = chip * CORES + lax.rem(i + c + 1, CORES)
             low_send[to] = lowest(to)
             m_copy(to, me_p).start()
 

time: 84.5 us -> 84.3 us (level)
  no operation moved by 1% of the time
where the time goes in v8:
time: 84.3 us; the launch traced here: 84.1 us
  Pallas kernels  80.6 us (96%)
  local copies, waits for them, and re-layouts  2.91 us (3%)
    pallas_call x1, Pallas kernels, per_device(): pl.pallas_call(functools.partial(body, nx, ny, nz), out_shape=(jax.ShapeD...  80.6 us
    unnamed x7, local copies, waits for them, and re-layouts  2.91 us

profile of v8, /device:TPU:1, one launch (start us, length us, event | category | flops | bytes accessed | tf_op | source)
XLA Modules:
  0.0 84.1 jit_solution(978409048425190876)
XLA Ops:
  0.6 80.6 %shard_map.94 = (f32[512,128]{1,0:T(8,128)}, f32[4,128]{1,0:T(4,128)}, f32[2,128]{1,0:T(2,128)}) custom-call(bf16[512,128]{1,0:T(8,128)(2,1)} %lat_in.1, s32[1,512]{1,0:T(1,128)} %bitcast.6, s32[1,32]{1,0:T(1,128)} %bitcast.10, s32[1,32]{1,0:T(1,128)} %bitcast.11, f32[512,128]{1,0:T(8,128)} %ema_s_in.1, f32[4,128]{1,0:T(4,128)} %bitcast.7, ...), custom_call_target="tpu_custom_call" | custom-call | tf_op jit(solution)/shard_map/pallas_call | solution.py:497
  81.2 0.0 copy-start
  81.2 1.7 %copy.13 = f32[512,128]{1,0:T(8,128)} copy(f32[512,128]{1,0:T(8,128)} %get-tuple-element.12) | data formatting | bytes 524288
  82.9 0.0 copy-done
  82.9 0.0 copy-start.1
  82.9 0.6 copy.14
  83.5 0.1 copy-done.1
  83.5 0.6 copy.15
Async XLA Ops:
  81.2 1.7 %copy-start = (f32[4,128]{1,0:T(4,128)S(1)}, f32[4,128]{1,0:T(4,128)}, u32[]{:S(2)}) copy-start(f32[4,128]{1,0:T(4,128)} %get-tuple-element.7) | copy-start | bytes 6148
  82.9 0.7 copy-start.1

commit v9 on v8

--- a/solution.py
+++ b/solution.py
@@ -25,8 +25,8 @@
 
 
 def body(
-    nx, ny, nz, lat_in, ids_in, dead_in, ridx_in, ema_s_in, ema_c_in, nxt_in, book, cnt_out, dist,
-    lat, ids, dead, ridx, ema_s, ema_c, nxt, turned,
+    nx, ny, nz, lat_in, ids_in, dead_in, ridx_in, ema_s_in, ema_c_in, nxt_in, book_hbm, cnt_hbm, dist,
+    book, cnt_out, lat, ids, dead, ridx, ema_s, ema_c, nxt, turned,
     pack, zbuf, relay, gsrc, gbuf, qbuf, ext, parts, rs_send, rs_recv, code, norm, acc, low_send, low_recv, cnts, in_s,
     z_s, z_r, relay_s, relay_r, g_s, g_r, q1_s, q1_r, q2_s, q2_r, q3_s, q3_r, f_s, f_r, x_s, x_r, b_s, b_r, c_s, c_r,
     right_s, right_r, left_s, left_r, m_s, m_r,
@@ -295,7 +295,7 @@
         )
 
     tags, got = arrived(3)
-    for d in range(1, nx + 1):
+    for d in (nx // 2, *(i for i in range(1, nx) if i != nx // 2), nx):
         to = lax.rem(x + d, nx)
         scale = jnp.float32(1.0)
         for i in range(1, nx):
@@ -336,13 +336,13 @@
     def right(r, j):
         return pltpu.make_async_remote_copy(
             src_ref=code.at[jnp.maximum(4 * r - 2, 0)], dst_ref=code.at[4 * r + j],
-            send_sem=right_s, recv_sem=right_r.at[r], device_id=along_z(j), device_id_type=MESH,
+            send_sem=right_s, recv_sem=right_r.at[r, j - 1], device_id=along_z(j), device_id_type=MESH,
         )
 
     def left(r, j):
         return pltpu.make_async_remote_copy(
             src_ref=code.at[4 * r], dst_ref=code.at[4 * r + 2 + j],
-            send_sem=left_s, recv_sem=left_r.at[r], device_id=along_z(-j), device_id_type=MESH,
+            send_sem=left_s, recv_sem=left_r.at[r, j - 1], device_id=along_z(-j), device_id_type=MESH,
         )
 
     right(jnp.int32(0), 2).start()
@@ -423,9 +423,9 @@
 
     @pl.loop(0, rounds - 1)
     def _(t):
-        sent(code.at[0:2], right_r.at[t])
+        sent(code.at[0], right_r.at[t, 1])
         right(t + 1, 2).start()
-        sent(code.at[0:2], left_r.at[t])
+        sent(code.at[0], left_r.at[t, 1])
 
         @pl.when(t < rounds - 2)
         def _():
@@ -433,6 +433,8 @@
 
         right(t + 1, 1).start()
         left(t + 1, 1).start()
+        sent(code.at[0], right_r.at[t, 0])
+        sent(code.at[0], left_r.at[t, 0])
         norms(4 * t + 1, 4)
 
         @pl.loop(0, spread_out)
@@ -440,8 +442,19 @@
             compare(4 * t + 1, 4, o)
 
     last = 4 * (rounds - 1) + 1
-    sent(code.at[0:2], right_r.at[rounds - 1])
-    sent(code.at[0], left_r.at[rounds - 1])
+    sent(book.at[0 : (nx - 1) * sub], b_r)
+    sent(cnts.at[0 : nx - 1], c_r)
+    for i in range(nx):
+        cnt_out[i : i + 1, :] = cnts[i, 0:1, :]
+    results = [
+        pltpu.make_async_copy(book, book_hbm, in_s.at[0]),
+        pltpu.make_async_copy(cnt_out, cnt_hbm, in_s.at[1]),
+    ]
+    for result in results:
+        result.start()
+    sent(code.at[0], right_r.at[rounds - 1, 0])
+    sent(code.at[0], left_r.at[rounds - 1, 0])
+    sent(code.at[0], right_r.at[rounds - 1, 1])
     norms(last, 3)
 
     @pl.loop(0, spread_out)
@@ -464,10 +477,8 @@
         first = h * (8 // halves)
         dist[h : h + 1, :] = (best[first : first + 1] + query_norm[:, h * 128 : (h + 1) * 128]) / 128
 
-    sent(book.at[0 : (nx - 1) * sub], b_r)
-    sent(cnts.at[0 : nx - 1], c_r)
-    for i in range(nx):
-        cnt_out[i : i + 1, :] = cnts[i, 0:1, :]
+    for result in results:
+        result.wait()
 
     sent(pack.at[0 : nz - 1], z_s)
     sent(relay, relay_s)
@@ -502,8 +513,10 @@
             jax.ShapeDtypeStruct((queries // 128, 128), f32),
         ),
         in_specs=[hbm] * 7,
-        out_specs=(vmem,) * 3,
+        out_specs=(hbm, hbm, vmem),
         scratch_shapes=[
+            pltpu.VMEM((k_dev, 128), f32),
+            pltpu.VMEM((nx, sub), f32),
             pltpu.VMEM(latents.shape, bf16),
             pltpu.VMEM((1, code_ids.shape[0]), jnp.int32),
             pltpu.VMEM((1, dead_codes.shape[0]), jnp.int32),
@@ -533,7 +546,7 @@
             dma, dma((4,)),
             dma, dma, dma, dma, dma, dma, dma, dma,
             dma, dma, dma, dma, dma, dma,
-            dma, dma((nz // 4,)), dma, dma((nz // 4,)),
+            dma, dma((nz // 4, 2)), dma, dma((nz // 4, 2)),
             dma, dma,
         ],
         compiler_params=pltpu.CompilerParams(

time: 84.3 us -> 84.3 us (level)
  no operation moved by 1% of the time
where the time goes in v9:
time: 84.3 us; the launch traced here: 84.2 us
  Pallas kernels  80.6 us (96%)
  local copies, waits for them, and re-layouts  2.91 us (3%)
    pallas_call x1, Pallas kernels, per_device(): pl.pallas_call(functools.partial(body, nx, ny, nz), out_shape=(jax.ShapeD...  80.6 us
    unnamed x7, local copies, waits for them, and re-layouts  2.91 us

profile of v9, /device:TPU:1, one launch (start us, length us, event | category | flops | bytes accessed | tf_op | source)
XLA Modules:
  0.0 84.2 jit_solution(16425458939261637321)
XLA Ops:
  0.6 80.6 %shard_map.94 = (f32[512,128]{1,0:T(8,128)}, f32[4,128]{1,0:T(4,128)}, f32[2,128]{1,0:T(2,128)}) custom-call(bf16[512,128]{1,0:T(8,128)(2,1)} %lat_in.1, s32[1,512]{1,0:T(1,128)} %bitcast.6, s32[1,32]{1,0:T(1,128)} %bitcast.10, s32[1,32]{1,0:T(1,128)} %bitcast.11, f32[512,128]{1,0:T(8,128)} %ema_s_in.1, f32[4,128]{1,0:T(4,128)} %bitcast.7, ...), custom_call_target="tpu_custom_call" | custom-call | tf_op jit(solution)/shard_map/pallas_call | solution.py:508
  81.2 0.0 copy-start
  81.3 1.7 %copy.13 = f32[512,128]{1,0:T(8,128)} copy(f32[512,128]{1,0:T(8,128)} %get-tuple-element.12) | data formatting | bytes 524288
  82.9 0.0 copy-done
  82.9 0.0 copy-start.1
  82.9 0.6 copy.14
  83.5 0.1 copy-done.1
  83.6 0.6 copy.15
Async XLA Ops:
  81.2 1.7 %copy-start = (f32[4,128]{1,0:T(4,128)S(1)}, f32[4,128]{1,0:T(4,128)}, u32[]{:S(2)}) copy-start(f32[4,128]{1,0:T(4,128)} %get-tuple-element.7) | copy-start | bytes 6148
  82.9 0.7 copy-start.1

commit v10 on v9

--- a/solution.py
+++ b/solution.py
@@ -274,7 +274,8 @@
 
         @pl.loop(1, nyc)
         def _(d):
-            g_copy(g, lax.rem(me_yc + d, nyc)).start()
+            away = lax.rem(d + nyc // 2 - 2, nyc - 1) + 1
+            g_copy(g, lax.rem(me_yc + away, nyc)).start()
 
         gbuf[me_yc, pl.ds(g * group, group)] = gsrc[pl.ds(g * group, group), me_yc]
         if g > 0:
@@ -397,7 +398,7 @@
         both = 0.25 * jnp.sum(table * table, axis=1, keepdims=True)
         norm[0 : count * sub] = jnp.broadcast_to(both, (count * sub, 128))
 
-    def compare(first, count, o):
+    def compare(first, count, o, unroll):
         deep = count * sub
         for i in range(unroll):
             chip = lax.rem(me_chip + 1 + o * unroll + i, chips)
@@ -419,7 +420,7 @@
 
     @pl.loop(0, spread_out)
     def _(o):
-        compare(0, 1, o)
+        compare(0, 1, o, unroll)
 
     @pl.loop(0, rounds - 1)
     def _(t):
@@ -439,7 +440,7 @@
 
         @pl.loop(0, spread_out)
         def _(o):
-            compare(4 * t + 1, 4, o)
+            compare(4 * t + 1, 4, o, unroll)
 
     last = 4 * (rounds - 1) + 1
     sent(book.at[0 : (nx - 1) * sub], b_r)
@@ -457,11 +458,13 @@
     sent(code.at[0], right_r.at[rounds - 1, 1])
     norms(last, 3)
 
-    @pl.loop(0, spread_out)
+    few = 2
+
+    @pl.loop(0, chips // few)
     def _(o):
-        compare(last, 3, o)
-
-        @pl.loop(o * unroll * CORES, jnp.minimum((o + 1) * unroll * CORES, planes - 1))
+        compare(last, 3, o, few)
+
+        @pl.loop(o * few * CORES, jnp.minimum((o + 1) * few * CORES, planes - 1))
         def _(i):
             chip = lax.rem(me_chip + 1 + lax.div(i, CORES), chips)
             to = chip * CORES + lax.rem(i + c + 1, CORES)

time: 84.3 us -> 84.4 us (level)
  no operation moved by 1% of the time
where the time goes in v10:
time: 84.4 us; the launch traced here: 84.2 us
  Pallas kernels  80.7 us (96%)
  local copies, waits for them, and re-layouts  2.91 us (3%)
    pallas_call x1, Pallas kernels, per_device(): pl.pallas_call(functools.partial(body, nx, ny, nz), out_shape=(jax.ShapeD...  80.7 us
    unnamed x7, local copies, waits for them, and re-layouts  2.91 us

profile of v10, /device:TPU:1, one launch (start us, length us, event | category | flops | bytes accessed | tf_op | source)
XLA Modules:
  0.0 84.2 jit_solution(1250281410004092447)
XLA Ops:
  0.6 80.7 %shard_map.94 = (f32[512,128]{1,0:T(8,128)}, f32[4,128]{1,0:T(4,128)}, f32[2,128]{1,0:T(2,128)}) custom-call(bf16[512,128]{1,0:T(8,128)(2,1)} %lat_in.1, s32[1,512]{1,0:T(1,128)} %bitcast.6, s32[1,32]{1,0:T(1,128)} %bitcast.10, s32[1,32]{1,0:T(1,128)} %bitcast.11, f32[512,128]{1,0:T(8,128)} %ema_s_in.1, f32[4,128]{1,0:T(4,128)} %bitcast.7, ...), custom_call_target="tpu_custom_call" | custom-call | tf_op jit(solution)/shard_map/pallas_call | solution.py:511
  81.3 0.0 copy-start
  81.3 1.7 %copy.13 = f32[512,128]{1,0:T(8,128)} copy(f32[512,128]{1,0:T(8,128)} %get-tuple-element.12) | data formatting | bytes 524288
  83.0 0.0 copy-done
  83.0 0.0 copy-start.1
  83.0 0.6 copy.14
  83.6 0.1 copy-done.1
  83.6 0.6 copy.15
Async XLA Ops:
  81.3 1.7 %copy-start = (f32[4,128]{1,0:T(4,128)S(1)}, f32[4,128]{1,0:T(4,128)}, u32[]{:S(2)}) copy-start(f32[4,128]{1,0:T(4,128)} %get-tuple-element.7) | copy-start | bytes 6148
  83.0 0.7 copy-start.1
